TPU v7x, 128 devices: a whole 4x4x4 slice. The times are simulated.
128 devices in a mesh: kvp: 16 (over z, y), tp: 8 (over x, core).
Axes of the slice: x: 4, y: 4, z: 4, core: 2. Of those that a mesh axis runs over, the one named last changes fastest.
Arguments:
- hidden_in: bfloat16 [2, 128, 8192], P(None, None, 'kvp'), may hold values from -6 to 6
- w_query: bfloat16 [8192, 8192], P('kvp', 'tp'), may hold values from -0.0625 to 0.0625
- key_weight_matrix: bfloat16 [8192, 1024], P('kvp', 'tp'), may hold values from -0.0625 to 0.0625
- value_weight_matrix: bfloat16 [8192, 1024], P('kvp', 'tp'), may hold values from -0.0625 to 0.0625
- w_out: bfloat16 [8192, 8192], P('tp', 'kvp'), may hold values from -0.0625 to 0.0625
- paged_key_cache: bfloat16 [1024, 256, 1024], P('kvp', None, 'tp'), as said below
- paged_value_cache: bfloat16 [1024, 256, 1024], P('kvp', None, 'tp'), may hold values from -6 to 6
- block_request: int32 [1024], P('kvp'), may hold values from 0 to 127, as said below
- block_fill: int32 [1024], P('kvp'), may hold values from 1 to 256, as said below
- positions: int32 [128], replicated, may hold values from 0 to 1048576, as said below
Outputs:
- attn_out: bfloat16 [2, 128, 8192], P(None, None, 'kvp')
Inputs may be any that keep to these rules, and one draw needn't show every extreme that they name: `block_request`: each cache block belongs to one request; a request may own no block. `block_fill`: every block is full except the last block (highest index) of its request, which holds 1 to 256 live slots; some block of every draw is full and some holds one live slot. `paged_key_cache`: random keys, not derived from the projection. positions[0] is 1048576; for every other request r, positions[r] is 256 times the number of blocks of request r plus an offset below 256.
All inputs are finite; a program needn't handle non-finite values.
Results may differ from a plain program's by a relative error of at most 0.025.
Values may be sent and summed in bfloat16 or wider, within the bound.
No kernel may reach another device: no remote copies, remote signals or barrier semaphores. Data moves between devices by JAX's collectives and lax.ppermute only.
A program may use at most 128 MiB of HBM per device.

v0:
```python
import jax
import jax.numpy as jnp
from jax import lax
from jax.sharding import PartitionSpec as P

HEAD_SIZE = 128


floor_score = -1e30
rope_base = 500000.0


def combined_all(part, axis, combine):
    gathered = jax.tree.map(lambda a: lax.all_gather(a, axis), part)

    def take(source):
        return jax.tree.map(lambda a: lax.dynamic_index_in_dim(a, source, 0, False), gathered)

    return lax.fori_loop(
        1, lax.axis_size(axis), lambda source, state: combine(state, take(source)), take(0)
    )


def rotate_halves(vectors, position_slots):
    half_size = vectors.shape[-1] // 2
    inverse = rope_base ** (-(jnp.arange(half_size, dtype=jnp.float32) * 2.0 / vectors.shape[-1]))
    angles = position_slots.astype(jnp.float32)[..., None] * inverse
    cosine = jnp.cos(angles)[..., None, :]
    sine = jnp.sin(angles)[..., None, :]
    first_half = vectors[..., :half_size]
    second_half = vectors[..., half_size:]
    return jnp.concatenate(
        [first_half * cosine - second_half * sine, second_half * cosine + first_half * sine],
        axis=-1,
    )


def round_rows(query_projected, key_projected, value_projected, row_ids, positions, request_number):
    row_count = query_projected.shape[0]
    position_slots = positions[row_ids % request_number] + row_ids // request_number
    query_rows = (
        rotate_halves(query_projected.reshape(row_count, -1, HEAD_SIZE), position_slots)
        .astype(jnp.bfloat16)
        .reshape(row_count, -1)
    )
    keys_new = (
        rotate_halves(key_projected.reshape(row_count, -1, HEAD_SIZE), position_slots)
        .astype(jnp.bfloat16)
        .reshape(row_count, -1)
    )
    return (query_rows, keys_new, value_projected.astype(jnp.bfloat16))


def block_stats(chosen, block_keys, block_values, fill_count, scaling):
    scores = (
        jnp.einsum("snkgd,ntkd->nksgt", chosen, block_keys, preferred_element_type=jnp.float32)
        * scaling
    )
    live_slots = jnp.arange(block_keys.shape[1], dtype=jnp.int32)[None, :] < fill_count[:, None]
    scores = jnp.where(live_slots[:, None, None, None, :], scores, floor_score)
    largest_score = jnp.max(scores, axis=-1)
    weights = jnp.exp(scores - largest_score[..., None]).astype(jnp.bfloat16)
    running_totals = jnp.sum(weights.astype(jnp.float32), axis=-1)
    weighted_values = jnp.einsum(
        "nksgt,ntkd->nksgd", weights, block_values, preferred_element_type=jnp.float32
    )
    return (largest_score, running_totals, weighted_values)


def request_combine(largest_score, running_totals, weighted_values, owners, request_number):
    onehot = owners[:, None] == jnp.arange(request_number, dtype=jnp.int32)[None, :]
    best_score = jnp.max(
        jnp.where(onehot[:, :, None, None, None], largest_score[:, None], floor_score), axis=0
    )
    factor = jnp.exp(largest_score - best_score[owners])
    onefloat = onehot.astype(jnp.float32)
    total_req = jnp.einsum(
        "nr,nksg->rksg", onefloat, factor * running_totals, precision=lax.Precision.HIGHEST
    )
    summed_req = jnp.einsum(
        "nr,nksgd->rksgd",
        onefloat,
        factor[..., None] * weighted_values,
        precision=lax.Precision.HIGHEST,
    )
    return (best_score, total_req, summed_req)


def joined(first, second):
    peak_score = jnp.maximum(first[0], second[0])
    factor_a = jnp.exp(first[0] - peak_score)
    factor_b = jnp.exp(second[0] - peak_score)
    return (
        peak_score,
        first[1] * factor_a + second[1] * factor_b,
        first[2] * factor_a[..., None] + second[2] * factor_b[..., None],
    )


def finish(best_score, total_req, summed_req, query_rows, keys_new, values_new, scaling):
    decode_step_count = query_rows.shape[0]
    scores = (
        jnp.einsum("srkgd,trkd->rksgt", query_rows, keys_new, preferred_element_type=jnp.float32)
        * scaling
    )
    causal = jnp.arange(decode_step_count)[:, None] >= jnp.arange(decode_step_count)[None, :]
    scores = jnp.where(causal[None, None, :, None, :], scores, floor_score)
    peak_score = jnp.maximum(best_score, jnp.max(scores, axis=-1))
    factor = jnp.exp(best_score - peak_score)
    weights = jnp.exp(scores - peak_score[..., None]).astype(jnp.bfloat16)
    total_all = total_req * factor + jnp.sum(weights.astype(jnp.float32), axis=-1)
    summed_all = summed_req * factor[..., None] + jnp.einsum(
        "rksgt,trkd->rksgd", weights, values_new, preferred_element_type=jnp.float32
    )
    heads = (summed_all / total_all[..., None]).astype(jnp.bfloat16)
    return jnp.transpose(heads, (2, 0, 1, 3, 4)).reshape(decode_step_count, heads.shape[0], -1)


def local(
    hidden_in,
    w_query,
    key_weight_matrix,
    value_weight_matrix,
    w_out,
    paged_key_cache,
    paged_value_cache,
    block_request,
    block_fill,
    positions,
):
    decode_step_count, request_number, part_width = hidden_in.shape
    kv_heads = key_weight_matrix.shape[1] // HEAD_SIZE
    query_group = w_query.shape[1] // HEAD_SIZE // kv_heads
    scaling = HEAD_SIZE ** (-0.5)
    row_entries = hidden_in.reshape(decode_step_count * request_number, part_width)
    part_q = jnp.dot(row_entries, w_query, preferred_element_type=jnp.float32)
    part_k = jnp.dot(row_entries, key_weight_matrix, preferred_element_type=jnp.float32)
    part_v = jnp.dot(row_entries, value_weight_matrix, preferred_element_type=jnp.float32)
    query_projected, key_projected, value_projected = lax.psum((part_q, part_k, part_v), "kvp")
    row_ids = jnp.arange(decode_step_count * request_number, dtype=jnp.int32)
    query_rows, keys_new, values_new = round_rows(
        query_projected, key_projected, value_projected, row_ids, positions, request_number
    )
    query_rows = query_rows.reshape(
        decode_step_count, request_number, kv_heads, query_group, HEAD_SIZE
    )
    keys_new = keys_new.reshape(decode_step_count, request_number, kv_heads, HEAD_SIZE)
    values_new = values_new.reshape(decode_step_count, request_number, kv_heads, HEAD_SIZE)
    block_count = paged_key_cache.shape[0]
    block_keys = paged_key_cache.reshape(block_count, -1, kv_heads, HEAD_SIZE)
    block_values = paged_value_cache.reshape(block_count, -1, kv_heads, HEAD_SIZE)
    chosen = query_rows[:, block_request]
    largest_score, running_totals, weighted_values = block_stats(
        chosen, block_keys, block_values, block_fill, scaling
    )
    best_score, total_req, summed_req = request_combine(
        largest_score, running_totals, weighted_values, block_request, request_number
    )
    best_score, total_req, summed_req = combined_all(
        (best_score, total_req, summed_req), "kvp", joined
    )
    heads = finish(best_score, total_req, summed_req, query_rows, keys_new, values_new, scaling)
    partial_out = jnp.dot(
        heads.reshape(decode_step_count * request_number, -1),
        w_out,
        preferred_element_type=jnp.float32,
    )
    summed_out = lax.psum(partial_out, "tp")
    return summed_out.astype(jnp.bfloat16).reshape(decode_step_count, request_number, -1)


def solution(mesh):
    return jax.shard_map(
        local,
        mesh=mesh,
        in_specs=(
            P(None, None, "kvp"),
            P("kvp", "tp"),
            P("kvp", "tp"),
            P("kvp", "tp"),
            P("tp", "kvp"),
            P("kvp", None, "tp"),
            P("kvp", None, "tp"),
            P("kvp"),
            P("kvp"),
            P(),
        ),
        out_specs=P(None, None, "kvp"),
        check_vma=False,
    )
```

profile of v0, /device:TPU:1, one launch (start us, length us, event | category | flops | bytes accessed | tf_op | source)
XLA Modules:
  0.0 327.9 jit_solution(4089438667809389750)
XLA Ops:
  6.6 1.9 convolution_bitcast_fusion.1
  8.5 2.5 fusion.56
  11.1 0.7 compare_select_fusion.1
  11.8 1.9 gather_fusion
  13.9 0.3 multiply_cosine_fusion.1
  14.2 86.0 %all-reduce.5.cloned.1.call-done = (f32[256,8,128]{0,2,1:T(8,128)}, f32[256,1,128]{2,0,1:T(8,128)}) async-done(((f32[256,8,128]{0,2,1:T(8,128)}, f32[256,1,128]{2,0,1:T(8,128)}), (f32[256,8,128]{0,2,1:T(8,128)}, f32[256,1,128]{2,0,1:T(8,128)})) %all-reduce.5.cloned.1.call-update) | async-done | bytes 1179664 | tf_op jit(solution)/shard_map/psum | solution.py:139
  100.2 1.4 subtract_convert_fusion
  101.6 0.5 copy.115
  102.1 0.5 copy.116
  102.6 0.3 maximum_bitcast_fusion
  102.9 0.6 gather_fusion.1
  103.5 3.5 %fusion.54 = (f32[64,2,8]{2,1,0:T(2,128)S(1)}, f32[64,2,8,256]{3,2,1,0:T(8,128)S(1)}) fusion(bf16[64,256,128]{2,1,0:T(8,128)(2,1)} %param.17, bf16[64,2,8,128]{3,2,1,0:T(8,128)(2,1)S(1)} %gather_fusion.1, pred[64,256]{1,0:T(8,128)(4,1)S(1)} %iota_compare_fusion), kind=kOutput, calls=%fused_computation.96 | convolution fusion | flops 67894272 | bytes 5525504 | tf_op jit(solution)/shard_map/snkgd,ntkd->nksgt/dot_general | solution.py:56
  107.1 0.2 select_reduce_fusion
  107.3 0.4 convert_reduce_fusion
  107.8 0.7 gather_fusion.2
  108.5 3.0 fusion.18
  111.6 1.7 fusion.29
  113.4 0.2 fusion.57
  113.6 60.3 %all-reduce.6 = bf16[256,128]{1,0:T(8,128)(2,1)S(1)} all-reduce(f32[256,128]{1,0:T(8,128)S(1)} %fusion.57), channel_id=1, replica_groups=mesh['kvp'=16,'tp'=8] {'kvp'}, use_global_device_ids=true, to_apply=%region_8.9 | all-reduce | flops 32768 | bytes 196608 | tf_op jit(solution)/shard_map/psum | solution.py:139
  174.1 0.6 fusion.37
  174.8 0.5 copy.124
  175.3 0.5 copy.125
  175.8 17.7 %all-gather = f32[2048,2,8]{0,2,1:T(8,128)S(1)} all-gather(f32[128,2,8]{0,2,1:T(8,128)S(1)} %select_reduce_fusion), channel_id=2, replica_groups=mesh['kvp'=16,'tp'=8] {'kvp'}, dimensions={0}, use_global_device_ids=true | all-gather | bytes 139264 | tf_op jit(solution)/shard_map/all_gather | solution.py:14
  193.5 0.2 convolution_bitcast_fusion.2
  193.7 21.6 %all-gather.1 = f32[2048,2,8]{0,2,1:T(8,128)S(1)} all-gather(f32[128,2,8]{0,2,1:T(8,128)S(1)} %convolution_bitcast_fusion.2), channel_id=3, replica_groups=mesh['kvp'=16,'tp'=8] {'kvp'}, dimensions={0}, use_global_device_ids=true | all-gather | bytes 139264 | tf_op jit(solution)/shard_map/all_gather | solution.py:14
  215.3 2.6 fusion.55
  218.0 10.6 %all-gather.5.cloned.1.call-done = f32[2048,2,8,128]{3,0,2,1:T(8,128)} async-done(((f32[128,2,8,128]{3,0,2,1:T(8,128)}), f32[2048,2,8,128]{3,0,2,1:T(8,128)}) %all-gather.5.cloned.1.call-update) | async-done | bytes 16777232 | tf_op jit(solution)/shard_map/all_gather | solution.py:14
  228.6 1.3 slice_bitcast_fusion
  229.9 0.6 copy.120
  230.5 49.8 %while.19 = (s32[]{:T(128)}, f32[128,1,2,8]{0,3,2,1:T(8,128)S(1)}, f32[128,1,2,8]{0,3,2,1:T(8,128)S(1)}, f32[128,1,2,8,128]{4,3,2,1,0:T(8,128)S(1)}, f32[16,128,...) while((s32[]{:T(128)}, f32[128,1,2,8]{0,3,2,1:T(8,128)S(1)}, ...), condition=%wide.region_5.6_spmd, body=%wide.region_4.5_spmd.sunk | while | flops 800773 | bytes 5415059 | solution.py:19
  230.9 1.3 constant_dynamic-slice_fusion.5
  232.2 1.6 fusion.70
  234.2 1.3 constant_dynamic-slice_fusion.5
  235.6 1.6 fusion.70
  237.5 1.3 constant_dynamic-slice_fusion.5
  238.9 1.6 fusion.70
  240.9 1.3 constant_dynamic-slice_fusion.5
  242.2 1.6 fusion.70
  244.2 1.3 constant_dynamic-slice_fusion.5
  245.5 1.6 fusion.70
  247.5 1.3 constant_dynamic-slice_fusion.5
  248.8 1.6 fusion.70
  250.8 1.3 constant_dynamic-slice_fusion.5
  252.2 1.6 fusion.70
  254.1 1.3 constant_dynamic-slice_fusion.5
  255.5 1.6 fusion.70
  257.5 1.3 constant_dynamic-slice_fusion.5
  258.8 1.6 fusion.70
  260.8 1.3 constant_dynamic-slice_fusion.5
  262.1 1.6 fusion.70
  264.1 1.3 constant_dynamic-slice_fusion.5
  265.4 1.6 fusion.70
  267.4 1.3 constant_dynamic-slice_fusion.5
  268.8 1.6 fusion.70
  270.7 1.3 constant_dynamic-slice_fusion.5
  272.1 1.6 fusion.70
  274.1 1.3 constant_dynamic-slice_fusion.5
  275.4 1.6 fusion.70
  277.4 1.3 constant_dynamic-slice_fusion.5
  278.7 1.6 fusion.70
  280.7 0.5 convert_reduce_fusion.1
  281.4 1.2 fusion.21
  282.7 0.4 fusion.23
  283.1 38.0 %all-reduce.7 = bf16[256,512]{1,0:T(8,128)(2,1)} all-reduce(f32[256,512]{1,0:T(8,128)S(1)} %fusion.23), channel_id=1, replica_groups=mesh['kvp'=16,'tp'=8] {'tp'}, use_global_device_ids=true, to_apply=%region_10.11 | all-reduce | flops 131072 | bytes 786432 | tf_op jit(solution)/shard_map/psum | solution.py:168
  (135 shorter events, 6.5 us)
Async XLA Ops:
  6.5 2.0 copy-start
  6.5 7.2 %copy-start.6 = (s32[64]{0:T(128)S(1)}, s32[64]{0:T(128)}, u32[]{:S(2)}) copy-start(s32[64]{0:T(128)} %param.19) | copy-start | bytes 772
  6.5 5.3 %copy-start.1 = (s32[128]{0:T(128)S(1)}, s32[128]{0:T(128)}, u32[]{:S(2)}) copy-start(s32[128]{0:T(128)} %param.21) | copy-start | bytes 1540
  6.5 7.3 %copy-start.7 = (s32[64]{0:T(128)S(1)}, s32[64]{0:T(128)}, u32[]{:S(2)}) copy-start(s32[64]{0:T(128)} %param.20) | copy-start | bytes 772
  6.5 93.6 %all-reduce.5.cloned.1.call-start = ((), (), s32[]{:S(2)}) async-start(), calls=%async_computation.1 | async-start | bytes 2359296 | tf_op jit(solution)/shard_map/psum | solution.py:139
  11.1 217.5 %all-gather.5.cloned.1.call-start = ((), (), s32[]{:S(2)}) async-start(), calls=%async_computation | async-start | bytes 17825792 | tf_op jit(solution)/shard_map/all_gather | solution.py:14
  108.5 4.8 %copy-start.2 = (bf16[2,128,512]{2,1,0:T(8,128)(2,1)S(1)}, bf16[2,128,512]{2,1,0:T(8,128)(2,1)}, u32[]{:S(2)}) copy-start(bf16[2,128,512]{2,1,0:T(8,128)(2,1)} %param.12) | copy-start | bytes 786436
  108.5 4.8 %copy-start.5 = (bf16[512,128]{1,0:T(8,128)(2,1)S(1)}, bf16[512,128]{1,0:T(8,128)(2,1)}, u32[]{:S(2)}) copy-start(bf16[512,128]{1,0:T(8,128)(2,1)} %param.15) | copy-start | bytes 393220
  111.6 62.5 %copy-start.4 = (f32[256,1,128]{2,0,1:T(8,128)S(1)}, f32[256,1,128]{2,0,1:T(8,128)}, u32[]{:S(2)}) copy-start(f32[256,1,128]{2,0,1:T(8,128)} %get-tuple-element.243) | copy-start | bytes 393220
  281.4 1.3 copy-start.3
Sparse Core Ops, SparseCore 0:
  11.2 88.9 all-reduce.4
  113.5 115.0 all-gather.4
where the time goes:
time: 331 us; the launch traced here: 328 us
  blocking collectives  138 us (42%)
  waiting for transfers between devices  96.6 us (29%)
  local copies, waits for them, and re-layouts  32.4 us (10%)
  other arithmetic  28.9 us (9%)
  matrix products  17.4 us (5%)
  between operations  13.8 us (4%)
    psum x1, waiting for transfers between devices, local(): lax.psum((part_q, part_k, part_v), 'kvp')  86 us
    psum x1, blocking collectives, local(): lax.psum((part_q, part_k, part_v), 'kvp')  60.3 us
    all_gather x2, blocking collectives, combined_all(): gathered = jax.tree.map(lambda a: lax.all_gather(a, axis), part)  39.3 us
    psum x1, blocking collectives, local(): summed_out = lax.psum(partial_out, 'tp')  38 us
    add x15, other arithmetic, joined(): first[2] * factor_a[..., None] + second[2] * factor_b[..., None]  23.7 us
    dynamic_slice x30, local copies, waits for them, and re-layouts, take(): lax.dynamic_index_in_dim(a, source, 0, False)  20.2 us
    all_gather x1, waiting for transfers between devices, combined_all(): gathered = jax.tree.map(lambda a: lax.all_gather(a, axis), part)  10.6 us
  transfers between devices with their start and end apart: 2, of which 2 were waited for; matrix products, arithmetic and copies ran while one was open for 2% of the time, Pallas kernels for 0%

commit v1 on v0

v1 whole, which is shorter than its diff:
```python
import functools

import jax
import jax.numpy as jnp
from jax import lax
from jax.experimental import pallas as pl
from jax.experimental.pallas import tpu as pltpu
from jax.sharding import PartitionSpec as P

HEAD_SIZE = 128
STAT_ROWS = 16
PIECES = 3

floor_score = -1e30
rope_base = 500000.0
VMEM = pl.BlockSpec(memory_space=pltpu.VMEM)
NT = (((1,), (1,)), ((), ()))


def params(mib=24):
    return pltpu.CompilerParams(vmem_limit_bytes=mib * 1024 * 1024)


def rotation_tables(positions, first, count, steps):
    half = HEAD_SIZE // 2
    inverse = rope_base ** (-(jnp.arange(half, dtype=jnp.float32) * 2.0 / HEAD_SIZE))
    own = lax.dynamic_slice_in_dim(positions, first, count)
    slots = own[None, :] + jnp.arange(steps, dtype=jnp.int32)[:, None]
    angles = slots.reshape(-1).astype(jnp.float32)[:, None] * inverse
    cosine, sine = jnp.cos(angles), jnp.sin(angles)
    return (
        jnp.concatenate([cosine, cosine], axis=-1),
        jnp.concatenate([-sine, sine], axis=-1),
    )


def project_kernel(hidden_ref, wq_ref, wk_ref, wv_ref, out_ref):
    steps, requests, width = hidden_ref.shape
    owners, rows, _ = out_ref.shape
    own = rows // steps
    hidden = hidden_ref[...].reshape(steps * requests, width)
    column = 0
    for ref in (wq_ref, wk_ref, wv_ref):
        total = ref.shape[1]
        chunk = min(total, 256)
        for start in range(0, total, chunk):
            part = jnp.dot(
                hidden, ref[:, start : start + chunk], preferred_element_type=jnp.float32
            )
            split = [
                part[s * requests : (s + 1) * requests].reshape(owners, own, chunk)
                for s in range(steps)
            ]
            out_ref[:, :, column : column + chunk] = jnp.concatenate(split, axis=1).astype(
                jnp.bfloat16
            )
            column += chunk


def rotate_kernel(parts_ref, cos_ref, sin_ref, q_ref, new_ref, turned_ref):
    sources, rows, columns = parts_ref.shape
    steps = 2
    own = rows // steps
    group = columns // HEAD_SIZE - 2
    cosine, sine = cos_ref[...], sin_ref[...]

    def head(index):
        lanes = slice(index * HEAD_SIZE, (index + 1) * HEAD_SIZE)
        return jnp.sum(parts_ref[:, :, lanes].astype(jnp.float32), axis=0)

    def rope(x):
        return x * cosine + pltpu.roll(x, HEAD_SIZE // 2, 1) * sine

    for g in range(group):
        x = rope(head(g))
        for s in range(steps):
            turned_ref[pl.ds(s * group + g, own, stride=steps * group), :] = x[
                s * own : (s + 1) * own
            ]
    new_ref[0] = rope(head(group)).astype(jnp.bfloat16)
    new_ref[1] = head(group + 1).astype(jnp.bfloat16)
    queries = turned_ref[...].astype(jnp.bfloat16)
    for d in range(q_ref.shape[0]):
        q_ref[d] = queries


def pieces(x):
    out = []
    for _ in range(PIECES):
        part = x.astype(jnp.bfloat16).astype(jnp.float32)
        out.append(part)
        x = x - part
    return out


def attention_kernel(
    scaling, request_ref, fill_ref, q_ref, k_ref, v_ref, out_ref, max_ref, total_ref, sum_ref
):
    step = pl.program_id(0)
    blocks, slots, _ = k_ref.shape
    requests, rows, _ = q_ref.shape

    @pl.when(step == 0)
    def _():
        max_ref[...] = jnp.full_like(max_ref, floor_score)
        total_ref[...] = jnp.zeros_like(total_ref)
        sum_ref[...] = jnp.zeros_like(sum_ref)

    slot = lax.broadcasted_iota(jnp.int32, (rows, slots), 1)
    found = []
    for b in range(blocks):
        n = step * blocks + b
        owner = request_ref[n]
        scores = (
            lax.dot_general(q_ref[owner], k_ref[b], NT, preferred_element_type=jnp.float32)
            * scaling
        )
        scores = jnp.where(slot < fill_ref[n], scores, floor_score)
        largest = jnp.max(scores, axis=1, keepdims=True)
        weights = jnp.exp(scores - largest).astype(jnp.bfloat16)
        total = jnp.sum(weights.astype(jnp.float32), axis=1, keepdims=True)
        summed = jnp.dot(weights, v_ref[b], preferred_element_type=jnp.float32)
        found.append((owner, largest, total, summed))
    for owner, largest, total, summed in found:
        before = max_ref[owner]
        after = jnp.maximum(before, largest)
        keep = jnp.exp(before - after)
        add = jnp.exp(largest - after)
        max_ref[owner] = after
        total_ref[owner] = total_ref[owner] * keep + total * add
        sum_ref[owner] = sum_ref[owner] * keep + summed * add

    @pl.when(step == pl.num_programs(0) - 1)
    def _():
        owners = out_ref.shape[0]
        own = requests // owners
        flat = own * rows
        lane = lax.broadcasted_iota(jnp.int32, (flat, HEAD_SIZE), 1)
        pick = (
            lax.broadcasted_iota(jnp.int32, (STAT_ROWS, HEAD_SIZE), 0)
            == lax.broadcasted_iota(jnp.int32, (STAT_ROWS, HEAD_SIZE), 1)
        ).astype(jnp.bfloat16)
        for d in range(owners):
            mine = slice(d * own, (d + 1) * own)
            out_ref[d, :flat, :] = sum_ref[mine].reshape(flat, HEAD_SIZE).astype(jnp.bfloat16)
            values = pieces(max_ref[mine].reshape(flat, HEAD_SIZE)) + pieces(
                total_ref[mine].reshape(flat, HEAD_SIZE)
            )
            table = jnp.zeros((flat, HEAD_SIZE), jnp.float32)
            for i, value in enumerate(values):
                table = jnp.where(lane == i, value, table)
            out_ref[d, flat:, :] = lax.dot_general(
                pick, table.astype(jnp.bfloat16), NT, preferred_element_type=jnp.float32
            ).astype(jnp.bfloat16)


def finish_kernel(scaling, parts_ref, q_ref, new_ref, out_ref, heads_ref):
    sources = parts_ref.shape[0]
    flat = q_ref.shape[0]
    steps = 2
    own = new_ref.shape[1] // steps
    rows = flat // own
    group = rows // steps

    stats = parts_ref[:, flat:, :].astype(jnp.float32)
    largest = sum(stats[:, i, :] for i in range(PIECES))
    total = sum(stats[:, PIECES + i, :] for i in range(PIECES))
    pad = HEAD_SIZE - sources
    largest = jnp.concatenate([largest, jnp.full((pad, flat), floor_score, jnp.float32)], axis=0).T
    total = jnp.concatenate([total, jnp.zeros((pad, flat), jnp.float32)], axis=0).T

    def spread(x):
        return jnp.broadcast_to(x[:, None, :], (own, rows, HEAD_SIZE)).reshape(flat, HEAD_SIZE)

    queries = q_ref[...].astype(jnp.float32)
    keys = new_ref[0].astype(jnp.float32)
    values = new_ref[1].astype(jnp.float32)
    row = lax.broadcasted_iota(jnp.int32, (flat, 1), 0)
    row_step = (row % rows) // group
    scores = []
    for t in range(steps):
        score = (
            jnp.sum(queries * spread(keys[t * own : (t + 1) * own]), axis=1, keepdims=True)
            * scaling
        )
        scores.append(jnp.where(row_step >= t, score, floor_score))
    peak = jnp.max(largest, axis=1, keepdims=True)
    for score in scores:
        peak = jnp.maximum(peak, score)
    factor = jnp.exp(largest - peak)
    weight_total = jnp.sum(factor * total, axis=1, keepdims=True)
    summed = jnp.zeros((flat, HEAD_SIZE), jnp.float32)
    for source in range(sources):
        summed = summed + factor[:, source : source + 1] * parts_ref[source, :flat, :].astype(
            jnp.float32
        )
    for t in range(steps):
        weight = jnp.exp(scores[t] - peak).astype(jnp.bfloat16).astype(jnp.float32)
        weight_total = weight_total + weight
        summed = summed + weight * spread(values[t * own : (t + 1) * own])
    heads_ref[...] = summed / weight_total
    columns = []
    for g in range(group):
        columns.append(
            jnp.concatenate(
                [
                    heads_ref[pl.ds(s * group + g, own, stride=rows), :]
                    for s in range(steps)
                ],
                axis=0,
            )
        )
    heads = jnp.concatenate(columns, axis=1).astype(jnp.bfloat16)
    for d in range(out_ref.shape[0]):
        out_ref[d] = heads


def output_kernel(core_ref, heads_ref, w_ref, keep_ref, send_ref):
    owners, rows, width = heads_ref.shape
    steps = 2
    own = rows // steps
    core = core_ref[0]
    heads = heads_ref[...].reshape(owners * rows, width)
    columns = w_ref.shape[1]
    chunk = min(columns, 256)
    for start in range(0, columns, chunk):
        lanes = slice(start, start + chunk)
        part = jnp.dot(heads, w_ref[:, lanes], preferred_element_type=jnp.float32)
        part = part.reshape(owners, rows, chunk)
        first = part[:, :own].reshape(owners * own, chunk)
        second = part[:, own:].reshape(owners * own, chunk)
        keep_ref[:, lanes] = jnp.where(core == 0, first, second)
        send_ref[:, lanes] = jnp.where(core == 0, second, first).astype(jnp.bfloat16)


def local(
    hidden_in,
    w_query,
    key_weight_matrix,
    value_weight_matrix,
    w_out,
    paged_key_cache,
    paged_value_cache,
    block_request,
    block_fill,
    positions,
):
    bf16, f32 = jnp.bfloat16, jnp.float32
    steps, requests, _ = hidden_in.shape
    group = w_query.shape[1] // HEAD_SIZE
    owners = lax.axis_size("kvp")
    own = requests // owners
    rows = steps * own
    flat = rows * group
    scaling = HEAD_SIZE ** (-0.5)
    blocks, slots, _ = paged_key_cache.shape
    out_columns = w_out.shape[1]

    def exchange(x):
        return lax.all_to_all(x, "kvp", 0, 0, tiled=True)

    cosine, sine = rotation_tables(positions, lax.axis_index("kvp") * own, own, steps)
    columns = (group + 2) * HEAD_SIZE
    parts = pl.pallas_call(
        project_kernel,
        out_shape=jax.ShapeDtypeStruct((owners, rows, columns), bf16),
        in_specs=[VMEM] * 4,
        out_specs=VMEM,
        compiler_params=params(),
    )(hidden_in, w_query, key_weight_matrix, value_weight_matrix)
    parts = exchange(parts)
    queries, new_rows = pl.pallas_call(
        rotate_kernel,
        out_shape=(
            jax.ShapeDtypeStruct((owners, flat, HEAD_SIZE), bf16),
            jax.ShapeDtypeStruct((2, rows, HEAD_SIZE), bf16),
        ),
        in_specs=[VMEM] * 3,
        out_specs=(VMEM, VMEM),
        scratch_shapes=[pltpu.VMEM((flat, HEAD_SIZE), f32)],
        compiler_params=params(),
    )(parts, cosine, sine)
    own_queries = queries[0]
    queries = exchange(queries).reshape(requests, steps * group, HEAD_SIZE)

    per_step = 8
    sums = (requests, steps * group, HEAD_SIZE)
    parts = pl.pallas_call(
        functools.partial(attention_kernel, scaling),
        out_shape=jax.ShapeDtypeStruct((owners, flat + STAT_ROWS, HEAD_SIZE), bf16),
        grid_spec=pltpu.PrefetchScalarGridSpec(
            num_scalar_prefetch=2,
            grid=(blocks // per_step,),
            in_specs=[
                pl.BlockSpec(sums, lambda i, *_: (0, 0, 0)),
                pl.BlockSpec((per_step, slots, HEAD_SIZE), lambda i, *_: (i, 0, 0)),
                pl.BlockSpec((per_step, slots, HEAD_SIZE), lambda i, *_: (i, 0, 0)),
            ],
            out_specs=pl.BlockSpec(
                (owners, flat + STAT_ROWS, HEAD_SIZE), lambda i, *_: (0, 0, 0)
            ),
            scratch_shapes=[pltpu.VMEM(sums, f32)] * 3,
        ),
        compiler_params=params(),
    )(block_request, block_fill, queries, paged_key_cache, paged_value_cache)
    parts = exchange(parts)
    heads = pl.pallas_call(
        functools.partial(finish_kernel, scaling),
        out_shape=jax.ShapeDtypeStruct((owners, rows, group * HEAD_SIZE), bf16),
        in_specs=[VMEM] * 3,
        out_specs=VMEM,
        scratch_shapes=[pltpu.VMEM((flat, HEAD_SIZE), f32)],
        compiler_params=params(),
    )(parts, own_queries, new_rows)
    heads = exchange(heads)

    tp = lax.axis_index("tp")
    core = tp % 2
    half = (owners * own, out_columns)
    keep, send = pl.pallas_call(
        output_kernel,
        out_shape=(jax.ShapeDtypeStruct(half, f32), jax.ShapeDtypeStruct(half, bf16)),
        in_specs=[pl.BlockSpec(memory_space=pltpu.SMEM), VMEM, VMEM],
        out_specs=(VMEM, VMEM),
        compiler_params=params(),
    )(core.reshape(1), heads, w_out)

    devices = lax.axis_size("tp")

    def swap(x, bits):
        return lax.ppermute(x, "tp", [(i, i ^ bits) for i in range(devices)])

    mine = (keep + swap(send, 1).astype(f32)).astype(bf16)
    others = [swap(mine, bits) for bits in (2, 6, 4)]
    near, across, far = (x.astype(f32) for x in others)
    mine = ((mine.astype(f32) + near) + (across + far)).astype(bf16)
    other = swap(mine, 1)
    return jnp.where(core == 0, jnp.stack([mine, other]), jnp.stack([other, mine]))


def solution(mesh):
    return jax.shard_map(
        local,
        mesh=mesh,
        in_specs=(
            P(None, None, "kvp"),
            P("kvp", "tp"),
            P("kvp", "tp"),
            P("kvp", "tp"),
            P("tp", "kvp"),
            P("kvp", None, "tp"),
            P("kvp", None, "tp"),
            P("kvp"),
            P("kvp"),
            P(),
        ),
        out_specs=P(None, None, "kvp"),
        check_vma=False,
    )
```

time: 331 us -> 109 us (0.33)
  blocking collectives: 138 us -> 14 us
  waiting for transfers between devices: 96.6 us -> 37.4 us
  other arithmetic: 28.9 us -> 1.04 us
  starting transfers between devices: 0.08 us -> 24.8 us
  local copies, waits for them, and re-layouts: 32.4 us -> 9.19 us
  Pallas kernels: 0 us -> 22.2 us
  matrix products: 17.4 us -> 0 us
  between operations: 13.8 us -> 0.09 us
    psum x2 -> x0, blocking collectives: 98.3 us -> none  [the longest x1 60.3 us: local(): lax.psum((part_q, part_k, part_v), 'kvp')]
    psum x1 -> x0, waiting for transfers between devices: 86 us -> none  [local(): lax.psum((part_q, part_k, part_v), 'kvp')]
    all_gather x2 -> x0, blocking collectives: 39.3 us -> none  [combined_all(): gathered = jax.tree.map(lambda a: lax.all_gather(a, axis), part)]
    all_to_all x0 -> x3, waiting for transfers between devices: none -> 29.9 us  [exchange(): return lax.all_to_all(x, 'kvp', 0, 0, tiled=True)]
    add x15 -> x0, other arithmetic: 23.7 us -> none  [joined(): first[2] * factor_a[..., None] + second[2] * factor_b[..., None]]
    pallas_call x0 -> x5, Pallas kernels: none -> 22.2 us  [the longest x1 18.4 us: local(): pl.pallas_call(functools.partial(attention_kernel, scaling), out_shape=ja...]
    dynamic_slice x30 -> x1, local copies, waits for them, and re-layouts: 20.2 us -> 0.73 us  [rotation_tables(): own = lax.dynamic_slice_in_dim(positions, first, count)]
    all_to_all x0 -> x3, starting transfers between devices: none -> 15.8 us  [exchange(): return lax.all_to_all(x, 'kvp', 0, 0, tiled=True)]
  transfers between devices with their start and end apart: 2 -> 8, of which waited for: 2 -> 8; matrix products, arithmetic and copies ran while one was open for 2% -> 1% of each run, Pallas kernels for 0% -> 0%
where the time goes in v1:
time: 109 us
  waiting for transfers between devices  37.4 us (34%)
  starting transfers between devices  24.8 us (23%)
  Pallas kernels  22.2 us (20%)
  blocking collectives  14 us (13%)
  local copies, waits for them, and re-layouts  9.19 us (8%)
    all_to_all x3, waiting for transfers between devices, exchange(): return lax.all_to_all(x, 'kvp', 0, 0, tiled=True)  29.9 us
    pallas_call x1, Pallas kernels, local(): pl.pallas_call(functools.partial(attention_kernel, scaling), out_shape=ja...  18.4 us
    all_to_all x3, starting transfers between devices, exchange(): return lax.all_to_all(x, 'kvp', 0, 0, tiled=True)  15.8 us
    all_to_all x1, blocking collectives, exchange(): return lax.all_to_all(x, 'kvp', 0, 0, tiled=True)  14 us
    ppermute x5, starting transfers between devices, swap(): return lax.ppermute(x, 'tp', [(i, i ^ bits) for i in range(devices)])  9.1 us
    unnamed x18, local copies, waits for them, and re-layouts  8.37 us
    ppermute x5, waiting for transfers between devices, swap(): return lax.ppermute(x, 'tp', [(i, i ^ bits) for i in range(devices)])  7.51 us
  transfers between devices with their start and end apart: 8, of which 8 were waited for; matrix products, arithmetic and copies ran while one was open for 1% of the time, Pallas kernels for 0%

profile of v1, /device:TPU:1, one launch (start us, length us, event | category | flops | bytes accessed | tf_op | source)
XLA Modules:
  0.0 108.8 jit_solution(10884884763465257054)
XLA Ops:
  0.0 0.0 copy-start.2
  0.0 1.2 %copy-done.2 = bf16[512,1024]{1,0:T(8,128)(2,1)S(1)} copy-done((bf16[512,1024]{1,0:T(8,128)(2,1)S(1)}, bf16[512,1024]{1,0:T(8,128)(2,1)}, u32[]{:S(2)}) %copy-start.2) | copy-done | bytes 1048600
  1.2 0.0 copy-start.4
  1.2 0.9 copy-done.4
  2.2 0.0 copy-start.5
  2.2 0.9 copy-done.5
  3.1 0.0 copy-start.6
  3.1 0.9 copy-done.6
  4.0 0.0 copy-start.7
  4.0 0.0 copy-start.8
  4.0 1.4 %shard_map.100 = bf16[16,16,1280]{2,1,0:T(8,128)(2,1)} custom-call(bf16[2,128,512]{2,1,0:T(8,128)(2,1)S(1)} %copy-done.4, bf16[512,1024]{1,0:T(8,128)(2,1)S(1)} %copy-done.2, bf16[512,128]{1,0:T(8,128)(2,1)S(1)} %copy-done.5, bf16[512,128]{1,0:T(8,128)(2,1)S(1)} %copy-done.6), custom_call_target="tpu_custom_call" | custom-call | tf_op jit(solution)/shard_map/pallas_call | solution.py:264
  5.4 8.6 %all-to-all-start = ((bf16[16,16,1280]{2,1,0:T(8,128)(2,1)}), bf16[16,16,1280]{2,1,0:T(8,128)(2,1)S(1)}, u32[]{:S(2)}, u32[]{:S(2)}) async-start(bf16[16,16,1280]{2,1,0:T(8,128)(2,1)} %shard_map.100), calls=%async_computation | async-start | bytes 1310720 | tf_op jit(solution)/shard_map/all_to_all | solution.py:260
  14.0 0.7 dynamic_slice.3
  14.8 0.1 convert_element_type.32
  14.9 0.1 fusion
  15.0 0.1 pad_maximum_fusion
  15.1 10.7 %all-to-all-done.parts_ref = bf16[16,16,1280]{2,1,0:T(8,128)(2,1)S(1)} async-done(((bf16[16,16,1280]{2,1,0:T(8,128)(2,1)}), bf16[16,16,1280]{2,1,0:T(8,128)(2,1)S(1)}, u32[]{:S(2)}, u32[]{:S(2)}) %all-to-all-start) | async-done | bytes 655392 | tf_op jit(solution)/shard_map/all_to_all | solution.py:260
  25.8 0.2 shard_map.101
  26.0 14.0 %all_to_all.20 = bf16[16,128,128]{2,1,0:T(8,128)(2,1)S(1)} all-to-all(bf16[16,128,128]{2,1,0:T(8,128)(2,1)S(1)} %get-tuple-element.9), channel_id=1, replica_groups=mesh['kvp'=16,'tp'=8] {'kvp'}, dimensions={0} | all-to-all | bytes 1048576 | tf_op jit(solution)/shard_map/all_to_all | solution.py:260
  40.0 0.0 copy-done.7
  40.0 0.0 copy-done.8
  40.0 0.0 copy-start
  40.0 2.2 %copy-done = bf16[64,256,128]{2,1,0:T(8,128)(2,1)S(1)} copy-done((bf16[64,256,128]{2,1,0:T(8,128)(2,1)S(1)}, bf16[64,256,128]{2,1,0:T(8,128)(2,1)}, u32[]{:S(2)}) %copy-start) | copy-done | bytes 4194328
  42.2 0.0 copy-start.1
  42.2 2.2 %copy-done.1 = bf16[64,256,128]{2,1,0:T(8,128)(2,1)S(1)} copy-done((bf16[64,256,128]{2,1,0:T(8,128)(2,1)S(1)}, bf16[64,256,128]{2,1,0:T(8,128)(2,1)}, u32[]{:S(2)}) %copy-start.1) | copy-done | bytes 4194328
  44.4 0.0 copy-start.3
  44.4 18.4 %shard_map.102 = bf16[16,144,128]{2,1,0:T(8,128)(2,1)} custom-call(s32[64]{0:T(128)S(1)} %copy-done.7, s32[64]{0:T(128)S(1)} %copy-done.8, bf16[128,16,128]{2,1,0:T(8,128)(2,1)S(1)} %bitcast.6, bf16[64,256,128]{2,1,0:T(8,128)(2,1)S(1)} %copy-done, bf16[64,256,128]{2,1,0:T(8,128)(2,1)S(1)} %copy-done.1), custom_call_target="tpu_custom_call" | custom-call | tf_op jit(solution)/shard_map/pallas_call | solution.py:288
  62.8 3.6 %all-to-all-start.2 = ((bf16[16,144,128]{2,1,0:T(8,128)(2,1)}), bf16[16,144,128]{2,1,0:T(8,128)(2,1)S(1)}, u32[]{:S(2)}, u32[]{:S(2)}) async-start(bf16[16,144,128]{2,1,0:T(8,128)(2,1)} %shard_map.102), calls=%async_computation.2 | async-start | bytes 1179648 | tf_op jit(solution)/shard_map/all_to_all | solution.py:260
  66.4 10.2 %all-to-all-done.2.parts_ref = bf16[16,144,128]{2,1,0:T(8,128)(2,1)S(1)} async-done(((bf16[16,144,128]{2,1,0:T(8,128)(2,1)}), bf16[16,144,128]{2,1,0:T(8,128)(2,1)S(1)}, u32[]{:S(2)}, u32[]{:S(2)}) %all-to-all-start.2) | async-done | bytes 589856 | tf_op jit(solution)/shard_map/all_to_all | solution.py:260
  76.6 1.7 %shard_map.103 = bf16[16,16,1024]{2,1,0:T(8,128)(2,1)} custom-call(bf16[16,144,128]{2,1,0:T(8,128)(2,1)S(1)} %all-to-all-done.2.parts_ref, bf16[128,128]{1,0:T(8,128)(2,1)S(1)} %slice_bitcast_fusion.q_ref, bf16[2,16,128]{2,1,0:T(8,128)(2,1)S(1)} %get-tuple-element.10.new_ref), custom_call_target="tpu_custom_call" | custom-call | tf_op jit(solution)/shard_map/pallas_call | solution.py:307
  78.4 3.6 %all-to-all-start.3 = ((bf16[16,16,1024]{2,1,0:T(8,128)(2,1)}), bf16[16,16,1024]{2,1,0:T(8,128)(2,1)S(1)}, u32[]{:S(2)}, u32[]{:S(2)}) async-start(bf16[16,16,1024]{2,1,0:T(8,128)(2,1)} %shard_map.103), calls=%async_computation.3 | async-start | bytes 1048576 | tf_op jit(solution)/shard_map/all_to_all | solution.py:260
  81.9 8.9 %all-to-all-done.3.heads_ref = bf16[16,16,1024]{2,1,0:T(8,128)(2,1)S(1)} async-done(((bf16[16,16,1024]{2,1,0:T(8,128)(2,1)}), bf16[16,16,1024]{2,1,0:T(8,128)(2,1)S(1)}, u32[]{:S(2)}, u32[]{:S(2)}) %all-to-all-start.3) | async-done | bytes 524320 | tf_op jit(solution)/shard_map/all_to_all | solution.py:260
  90.9 0.0 copy-done.3
  90.9 0.4 shard_map.104
  91.3 4.2 %collective-permute-start = (bf16[128,512]{1,0:T(8,128)(2,1)S(1)}, bf16[128,512]{1,0:T(8,128)(2,1)S(1)}, u32[]{:S(2)}, u32[]{:S(2)}) collective-permute-start(bf16[128,512]{1,0:T(8,128)(2,1)S(1)} %get-tuple-element.12), channel_id=1, source_target_pairs={{0,1},{1,0},{2,3},{3,2},{4,5},{5,4},{6,7},{7,6},{8,9},{9,8},{10,11... | collective-permute-start | bytes 393224 | tf_op jit(solution)/shard_map/ppermute | solution.py:331
  95.5 1.0 collective-permute-done
  96.5 2.8 %collective-permute-start.3 = (bf16[128,512]{1,0:T(8,128)(2,1)S(1)}, bf16[128,512]{1,0:T(8,128)(2,1)S(1)}, u32[]{:S(2)}, u32[]{:S(2)}) collective-permute-start(bf16[128,512]{1,0:T(8,128)(2,1)S(1)} %add_convert_fusion.1), channel_id=1, source_target_pairs={{0,4},{1,5},{2,6},{3,7},{4,0},{5,1},{6,2},{7,3},{8,12},{9,13},{10,... | collective-permute-start | bytes 393224 | tf_op jit(solution)/shard_map/ppermute | solution.py:331
  99.3 0.9 collective-permute-start.2
  100.2 0.0 collective-permute-start.1
  100.2 2.6 %collective-permute-done.3 = bf16[128,512]{1,0:T(8,128)(2,1)S(1)} collective-permute-done((bf16[128,512]{1,0:T(8,128)(2,1)S(1)}, bf16[128,512]{1,0:T(8,128)(2,1)S(1)}, u32[]{:S(2)}, u32[]{:S(2)}) %collective-permute-start.3) | collective-permute-done | bytes 131104 | tf_op jit(solution)/shard_map/ppermute | solution.py:331
  102.8 2.8 %collective-permute-done.2 = bf16[128,512]{1,0:T(8,128)(2,1)S(1)} collective-permute-done((bf16[128,512]{1,0:T(8,128)(2,1)S(1)}, bf16[128,512]{1,0:T(8,128)(2,1)S(1)}, u32[]{:S(2)}, u32[]{:S(2)}) %collective-permute-start.2) | collective-permute-done | bytes 131104 | tf_op jit(solution)/shard_map/ppermute | solution.py:331
  105.7 0.1 collective-permute-done.1
  105.7 0.1 add_convert_fusion
  105.8 1.2 %collective-permute-start.4 = (bf16[128,512]{1,0:T(8,128)(2,1)S(1)}, bf16[128,512]{1,0:T(8,128)(2,1)S(1)}, u32[]{:S(2)}, u32[]{:S(2)}) collective-permute-start(bf16[128,512]{1,0:T(8,128)(2,1)S(1)} %add_convert_fusion), channel_id=1, source_target_pairs={{0,1},{1,0},{2,3},{3,2},{4,5},{5,4},{6,7},{7,6},{8,9},{9,8},{10,11... | collective-permute-start | bytes 393224 | tf_op jit(solution)/shard_map/ppermute | solution.py:331
  107.1 1.0 collective-permute-done.4
  108.0 0.7 maximum_select_fusion
  (4 shorter events, 0.0 us)
Async XLA Ops:
  0.0 1.2 %copy-start.2 = (bf16[512,1024]{1,0:T(8,128)(2,1)S(1)}, bf16[512,1024]{1,0:T(8,128)(2,1)}, u32[]{:S(2)}) copy-start(bf16[512,1024]{1,0:T(8,128)(2,1)} %wq_ref.1) | copy-start | bytes 3145732
  1.2 0.9 copy-start.4
  2.2 0.9 copy-start.5
  3.1 0.9 copy-start.6
  4.0 36.0 %copy-start.7 = (s32[64]{0:T(128)S(1)}, s32[64]{0:T(128)}, u32[]{:S(2)}) copy-start(s32[64]{0:T(128)} %request_ref.1) | copy-start | bytes 772
  4.0 36.0 %copy-start.8 = (s32[64]{0:T(128)S(1)}, s32[64]{0:T(128)}, u32[]{:S(2)}) copy-start(s32[64]{0:T(128)} %fill_ref.1) | copy-start | bytes 772
  5.4 20.4 %all-to-all-start = ((bf16[16,16,1280]{2,1,0:T(8,128)(2,1)}), bf16[16,16,1280]{2,1,0:T(8,128)(2,1)S(1)}, u32[]{:S(2)}, u32[]{:S(2)}) async-start(bf16[16,16,1280]{2,1,0:T(8,128)(2,1)} %shard_map.100), calls=%async_computation | async-start | bytes 1310720 | tf_op jit(solution)/shard_map/all_to_all | solution.py:260
  40.0 2.2 %copy-start = (bf16[64,256,128]{2,1,0:T(8,128)(2,1)S(1)}, bf16[64,256,128]{2,1,0:T(8,128)(2,1)}, u32[]{:S(2)}) copy-start(bf16[64,256,128]{2,1,0:T(8,128)(2,1)} %k_ref.1) | copy-start | bytes 12582916
  42.2 2.2 %copy-start.1 = (bf16[64,256,128]{2,1,0:T(8,128)(2,1)S(1)}, bf16[64,256,128]{2,1,0:T(8,128)(2,1)}, u32[]{:S(2)}) copy-start(bf16[64,256,128]{2,1,0:T(8,128)(2,1)} %v_ref.1) | copy-start | bytes 12582916
  44.4 46.5 %copy-start.3 = (bf16[1024,512]{1,0:T(8,128)(2,1)S(1)}, bf16[1024,512]{1,0:T(8,128)(2,1)}, u32[]{:S(2)}) copy-start(bf16[1024,512]{1,0:T(8,128)(2,1)} %w_ref.1) | copy-start | bytes 3145732
  62.8 13.8 %all-to-all-start.2 = ((bf16[16,144,128]{2,1,0:T(8,128)(2,1)}), bf16[16,144,128]{2,1,0:T(8,128)(2,1)S(1)}, u32[]{:S(2)}, u32[]{:S(2)}) async-start(bf16[16,144,128]{2,1,0:T(8,128)(2,1)} %shard_map.102), calls=%async_computation.2 | async-start | bytes 1179648 | tf_op jit(solution)/shard_map/all_to_all | solution.py:260
  78.4 12.5 %all-to-all-start.3 = ((bf16[16,16,1024]{2,1,0:T(8,128)(2,1)}), bf16[16,16,1024]{2,1,0:T(8,128)(2,1)S(1)}, u32[]{:S(2)}, u32[]{:S(2)}) async-start(bf16[16,16,1024]{2,1,0:T(8,128)(2,1)} %shard_map.103), calls=%async_computation.3 | async-start | bytes 1048576 | tf_op jit(solution)/shard_map/all_to_all | solution.py:260
  91.3 5.2 %collective-permute-start = (bf16[128,512]{1,0:T(8,128)(2,1)S(1)}, bf16[128,512]{1,0:T(8,128)(2,1)S(1)}, u32[]{:S(2)}, u32[]{:S(2)}) collective-permute-start(bf16[128,512]{1,0:T(8,128)(2,1)S(1)} %get-tuple-element.12), channel_id=1, source_target_pairs={{0,1},{1,0},{2,3},{3,2},{4,5},{5,4},{6,7},{7,6},{8,9},{9,8},{10,11... | collective-permute-start | bytes 393224 | tf_op jit(solution)/shard_map/ppermute | solution.py:331
  96.5 6.3 %collective-permute-start.3 = (bf16[128,512]{1,0:T(8,128)(2,1)S(1)}, bf16[128,512]{1,0:T(8,128)(2,1)S(1)}, u32[]{:S(2)}, u32[]{:S(2)}) collective-permute-start(bf16[128,512]{1,0:T(8,128)(2,1)S(1)} %add_convert_fusion.1), channel_id=1, source_target_pairs={{0,4},{1,5},{2,6},{3,7},{4,0},{5,1},{6,2},{7,3},{8,12},{9,13},{10,... | collective-permute-start | bytes 393224 | tf_op jit(solution)/shard_map/ppermute | solution.py:331
  99.3 6.3 %collective-permute-start.2 = (bf16[128,512]{1,0:T(8,128)(2,1)S(1)}, bf16[128,512]{1,0:T(8,128)(2,1)S(1)}, u32[]{:S(2)}, u32[]{:S(2)}) collective-permute-start(bf16[128,512]{1,0:T(8,128)(2,1)S(1)} %add_convert_fusion.1), channel_id=1, source_target_pairs={{0,6},{1,7},{2,4},{3,5},{4,2},{5,3},{6,0},{7,1},{8,14},{9,15},{10,... | collective-permute-start | bytes 393224 | tf_op jit(solution)/shard_map/ppermute | solution.py:331
  100.2 5.5 %collective-permute-start.1 = (bf16[128,512]{1,0:T(8,128)(2,1)S(1)}, bf16[128,512]{1,0:T(8,128)(2,1)S(1)}, u32[]{:S(2)}, u32[]{:S(2)}) collective-permute-start(bf16[128,512]{1,0:T(8,128)(2,1)S(1)} %add_convert_fusion.1), channel_id=1, source_target_pairs={{0,2},{1,3},{2,0},{3,1},{4,6},{5,7},{6,4},{7,5},{8,10},{9,11},{10,... | collective-permute-start | bytes 393224 | tf_op jit(solution)/shard_map/ppermute | solution.py:331
  105.8 2.2 %collective-permute-start.4 = (bf16[128,512]{1,0:T(8,128)(2,1)S(1)}, bf16[128,512]{1,0:T(8,128)(2,1)S(1)}, u32[]{:S(2)}, u32[]{:S(2)}) collective-permute-start(bf16[128,512]{1,0:T(8,128)(2,1)S(1)} %add_convert_fusion), channel_id=1, source_target_pairs={{0,1},{1,0},{2,3},{3,2},{4,5},{5,4},{6,7},{7,6},{8,9},{9,8},{10,11... | collective-permute-start | bytes 393224 | tf_op jit(solution)/shard_map/ppermute | solution.py:331

commit v2 on v1

--- a/solution.py
+++ b/solution.py
@@ -14,6 +14,8 @@
 floor_score = -1e30
 rope_base = 500000.0
 VMEM = pl.BlockSpec(memory_space=pltpu.VMEM)
+SMEM = pl.BlockSpec(memory_space=pltpu.SMEM)
+HBM = pl.BlockSpec(memory_space=pltpu.HBM)
 NT = (((1,), (1,)), ((), ()))
 
 
@@ -34,27 +36,36 @@
     )
 
 
-def project_kernel(hidden_ref, wq_ref, wk_ref, wv_ref, out_ref):
+def project_kernel(hidden_hbm, wq_hbm, wk_hbm, wv_hbm, out_ref, hidden_ref, w_ref, sems):
     steps, requests, width = hidden_ref.shape
-    owners, rows, _ = out_ref.shape
+    owners, rows, columns = out_ref.shape
     own = rows // steps
-    hidden = hidden_ref[...].reshape(steps * requests, width)
+    copies = [pltpu.make_async_copy(hidden_hbm, hidden_ref, sems.at[0])]
+    chunks = []
     column = 0
-    for ref in (wq_ref, wk_ref, wv_ref):
-        total = ref.shape[1]
+    for hbm in (wq_hbm, wk_hbm, wv_hbm):
+        total = hbm.shape[1]
         chunk = min(total, 256)
         for start in range(0, total, chunk):
-            part = jnp.dot(
-                hidden, ref[:, start : start + chunk], preferred_element_type=jnp.float32
+            lanes = slice(column, column + chunk)
+            copies.append(
+                pltpu.make_async_copy(
+                    hbm.at[:, start : start + chunk], w_ref.at[:, lanes], sems.at[len(copies)]
+                )
             )
-            split = [
-                part[s * requests : (s + 1) * requests].reshape(owners, own, chunk)
-                for s in range(steps)
-            ]
-            out_ref[:, :, column : column + chunk] = jnp.concatenate(split, axis=1).astype(
-                jnp.bfloat16
-            )
+            chunks.append(lanes)
             column += chunk
+    for copy in copies:
+        copy.start()
+    copies[0].wait()
+    hidden = hidden_ref[...].reshape(steps * requests, width)
+    for copy, lanes in zip(copies[1:], chunks):
+        copy.wait()
+        part = jnp.dot(hidden, w_ref[:, lanes], preferred_element_type=jnp.float32)
+        split = [
+            part[s * requests : (s + 1) * requests].reshape(owners, own, -1) for s in range(steps)
+        ]
+        out_ref[:, :, lanes] = jnp.concatenate(split, axis=1).astype(jnp.bfloat16)
 
 
 def rotate_kernel(parts_ref, cos_ref, sin_ref, q_ref, new_ref, turned_ref):
@@ -94,64 +105,107 @@
 
 
 def attention_kernel(
-    scaling, request_ref, fill_ref, q_ref, k_ref, v_ref, out_ref, max_ref, total_ref, sum_ref
+    scaling,
+    batch,
+    request_ref,
+    fill_ref,
+    q_ref,
+    k_hbm,
+    v_hbm,
+    out_ref,
+    k_ref,
+    v_ref,
+    max_ref,
+    total_ref,
+    sum_ref,
+    sems,
 ):
-    step = pl.program_id(0)
     blocks, slots, _ = k_ref.shape
     requests, rows, _ = q_ref.shape
-
-    @pl.when(step == 0)
-    def _():
-        max_ref[...] = jnp.full_like(max_ref, floor_score)
-        total_ref[...] = jnp.zeros_like(total_ref)
-        sum_ref[...] = jnp.zeros_like(sum_ref)
-
-    slot = lax.broadcasted_iota(jnp.int32, (rows, slots), 1)
-    found = []
-    for b in range(blocks):
-        n = step * blocks + b
-        owner = request_ref[n]
-        scores = (
-            lax.dot_general(q_ref[owner], k_ref[b], NT, preferred_element_type=jnp.float32)
-            * scaling
+    groups = blocks // batch
+    lanes = batch * rows
+
+    def load(hbm, ref, which, g):
+        span = pl.ds(g * batch, batch)
+        return pltpu.make_async_copy(hbm.at[span], ref.at[span], sems.at[which, g])
+
+    for g in range(groups):
+        load(k_hbm, k_ref, 0, g).start()
+        load(v_hbm, v_ref, 1, g).start()
+    max_ref[...] = jnp.full_like(max_ref, floor_score)
+    total_ref[...] = jnp.zeros_like(total_ref)
+    sum_ref[...] = jnp.zeros_like(sum_ref)
+
+    slot = lax.broadcasted_iota(jnp.int32, (slots, lanes), 0)
+    lane_block = lax.broadcasted_iota(jnp.int32, (1, lanes), 1) // rows
+    empty = jnp.zeros((rows, HEAD_SIZE), jnp.bfloat16)
+
+    def group_step(g, _):
+        first = g * batch
+        owners = [request_ref[first + b] for b in range(batch)]
+
+        def placed(b):
+            return jnp.concatenate(
+                [empty] * b + [q_ref[owners[b]]] + [empty] * (batch - b - 1), axis=0
+            )
+
+        load(k_hbm, k_ref, 0, g).wait()
+        scores = jnp.zeros((slots, lanes), jnp.float32)
+        for b in range(0, batch, 2):
+            scores = scores + lax.dot_general(
+                jnp.concatenate([k_ref[first + b], k_ref[first + b + 1]], axis=1),
+                jnp.concatenate([placed(b), placed(b + 1)], axis=1),
+                NT,
+                preferred_element_type=jnp.float32,
+            )
+        fill = jnp.zeros((1, lanes), jnp.int32)
+        for b in range(batch):
+            fill = jnp.where(lane_block == b, fill_ref[first + b], fill)
+        scores = jnp.where(slot < fill, scores * scaling, floor_score)
+        largest = jnp.max(scores, axis=0, keepdims=True)
+        weights = jnp.exp(scores - largest).astype(jnp.bfloat16).astype(jnp.float32)
+        total = jnp.sum(weights, axis=0, keepdims=True)
+        turned = weights.T.astype(jnp.bfloat16)
+        stats = jnp.concatenate(
+            [largest, total, jnp.zeros((6, lanes), jnp.float32)], axis=0
+        ).T
+        load(v_hbm, v_ref, 1, g).wait()
+        for b in range(batch):
+            mine = slice(b * rows, (b + 1) * rows)
+            summed = jnp.dot(turned[mine], v_ref[first + b], preferred_element_type=jnp.float32)
+            owner = owners[b]
+            before = max_ref[owner]
+            block_max = stats[mine, 0:1]
+            after = jnp.maximum(before, block_max)
+            keep = jnp.exp(before - after)
+            add = jnp.exp(block_max - after)
+            max_ref[owner] = after
+            total_ref[owner] = total_ref[owner] * keep + stats[mine, 1:2] * add
+            sum_ref[owner] = sum_ref[owner] * keep + summed * add
+        return 0
+
+    lax.fori_loop(0, groups, group_step, 0)
+
+    owners = out_ref.shape[0]
+    own = requests // owners
+    flat = own * rows
+    lane = lax.broadcasted_iota(jnp.int32, (flat, HEAD_SIZE), 1)
+    pick = (
+        lax.broadcasted_iota(jnp.int32, (STAT_ROWS, HEAD_SIZE), 0)
+        == lax.broadcasted_iota(jnp.int32, (STAT_ROWS, HEAD_SIZE), 1)
+    ).astype(jnp.bfloat16)
+    for d in range(owners):
+        mine = slice(d * own, (d + 1) * own)
+        out_ref[d, :flat, :] = sum_ref[mine].reshape(flat, HEAD_SIZE).astype(jnp.bfloat16)
+        values = pieces(max_ref[mine].reshape(flat, HEAD_SIZE)) + pieces(
+            total_ref[mine].reshape(flat, HEAD_SIZE)
         )
-        scores = jnp.where(slot < fill_ref[n], scores, floor_score)
-        largest = jnp.max(scores, axis=1, keepdims=True)
-        weights = jnp.exp(scores - largest).astype(jnp.bfloat16)
-        total = jnp.sum(weights.astype(jnp.float32), axis=1, keepdims=True)
-        summed = jnp.dot(weights, v_ref[b], preferred_element_type=jnp.float32)
-        found.append((owner, largest, total, summed))
-    for owner, largest, total, summed in found:
-        before = max_ref[owner]
-        after = jnp.maximum(before, largest)
-        keep = jnp.exp(before - after)
-        add = jnp.exp(largest - after)
-        max_ref[owner] = after
-        total_ref[owner] = total_ref[owner] * keep + total * add
-        sum_ref[owner] = sum_ref[owner] * keep + summed * add
-
-    @pl.when(step == pl.num_programs(0) - 1)
-    def _():
-        owners = out_ref.shape[0]
-        own = requests // owners
-        flat = own * rows
-        lane = lax.broadcasted_iota(jnp.int32, (flat, HEAD_SIZE), 1)
-        pick = (
-            lax.broadcasted_iota(jnp.int32, (STAT_ROWS, HEAD_SIZE), 0)
-            == lax.broadcasted_iota(jnp.int32, (STAT_ROWS, HEAD_SIZE), 1)
+        table = jnp.zeros((flat, HEAD_SIZE), jnp.float32)
+        for i, value in enumerate(values):
+            table = jnp.where(lane == i, value, table)
+        out_ref[d, flat:, :] = lax.dot_general(
+            pick, table.astype(jnp.bfloat16), NT, preferred_element_type=jnp.float32
         ).astype(jnp.bfloat16)
-        for d in range(owners):
-            mine = slice(d * own, (d + 1) * own)
-            out_ref[d, :flat, :] = sum_ref[mine].reshape(flat, HEAD_SIZE).astype(jnp.bfloat16)
-            values = pieces(max_ref[mine].reshape(flat, HEAD_SIZE)) + pieces(
-                total_ref[mine].reshape(flat, HEAD_SIZE)
-            )
-            table = jnp.zeros((flat, HEAD_SIZE), jnp.float32)
-            for i, value in enumerate(values):
-                table = jnp.where(lane == i, value, table)
-            out_ref[d, flat:, :] = lax.dot_general(
-                pick, table.astype(jnp.bfloat16), NT, preferred_element_type=jnp.float32
-            ).astype(jnp.bfloat16)
 
 
 def finish_kernel(scaling, parts_ref, q_ref, new_ref, out_ref, heads_ref):
@@ -264,8 +318,13 @@
     parts = pl.pallas_call(
         project_kernel,
         out_shape=jax.ShapeDtypeStruct((owners, rows, columns), bf16),
-        in_specs=[VMEM] * 4,
+        in_specs=[HBM] * 4,
         out_specs=VMEM,
+        scratch_shapes=[
+            pltpu.VMEM(hidden_in.shape, bf16),
+            pltpu.VMEM((hidden_in.shape[2], columns), bf16),
+            pltpu.SemaphoreType.DMA((group + 3,)),
+        ],
         compiler_params=params(),
     )(hidden_in, w_query, key_weight_matrix, value_weight_matrix)
     parts = exchange(parts)
@@ -283,25 +342,17 @@
     own_queries = queries[0]
     queries = exchange(queries).reshape(requests, steps * group, HEAD_SIZE)
 
-    per_step = 8
+    batch = 16
     sums = (requests, steps * group, HEAD_SIZE)
     parts = pl.pallas_call(
-        functools.partial(attention_kernel, scaling),
+        functools.partial(attention_kernel, scaling, batch),
         out_shape=jax.ShapeDtypeStruct((owners, flat + STAT_ROWS, HEAD_SIZE), bf16),
-        grid_spec=pltpu.PrefetchScalarGridSpec(
-            num_scalar_prefetch=2,
-            grid=(blocks // per_step,),
-            in_specs=[
-                pl.BlockSpec(sums, lambda i, *_: (0, 0, 0)),
-                pl.BlockSpec((per_step, slots, HEAD_SIZE), lambda i, *_: (i, 0, 0)),
-                pl.BlockSpec((per_step, slots, HEAD_SIZE), lambda i, *_: (i, 0, 0)),
-            ],
-            out_specs=pl.BlockSpec(
-                (owners, flat + STAT_ROWS, HEAD_SIZE), lambda i, *_: (0, 0, 0)
-            ),
-            scratch_shapes=[pltpu.VMEM(sums, f32)] * 3,
-        ),
-        compiler_params=params(),
+        in_specs=[SMEM, SMEM, VMEM, HBM, HBM],
+        out_specs=VMEM,
+        scratch_shapes=[pltpu.VMEM(paged_key_cache.shape, bf16)] * 2
+        + [pltpu.VMEM(sums, f32)] * 3
+        + [pltpu.SemaphoreType.DMA((2, blocks // batch))],
+        compiler_params=params(32),
     )(block_request, block_fill, queries, paged_key_cache, paged_value_cache)
     parts = exchange(parts)
     heads = pl.pallas_call(
@@ -320,7 +371,7 @@
     keep, send = pl.pallas_call(
         output_kernel,
         out_shape=(jax.ShapeDtypeStruct(half, f32), jax.ShapeDtypeStruct(half, bf16)),
-        in_specs=[pl.BlockSpec(memory_space=pltpu.SMEM), VMEM, VMEM],
+        in_specs=[SMEM, VMEM, VMEM],
         out_specs=(VMEM, VMEM),
         compiler_params=params(),
     )(core.reshape(1), heads, w_out)

time: 109 us -> 99.8 us (0.916)
  Pallas kernels: 22.2 us -> 12.5 us
    pallas_call x1, Pallas kernels: 18.4 us -> 7.45 us  [local(): pl.pallas_call(functools.partial(attention_kernel, scaling, batch), out_s...]
    pallas_call x1, Pallas kernels: 1.45 us -> 2.76 us  [local(): pl.pallas_call(project_kernel, out_shape=jax.ShapeDtypeStruct((owners, ro...]
  transfers between devices with their start and end apart: 8 -> 8, of which waited for: 8 -> 7; matrix products, arithmetic and copies ran while one was open for 1% -> 1% of each run, Pallas kernels for 0% -> 0%
where the time goes in v2:
time: 99.8 us; the launch traced here: 99.2 us
  waiting for transfers between devices  37.4 us (37%)
  starting transfers between devices  24.9 us (25%)
  blocking collectives  14 us (14%)
  Pallas kernels  12.5 us (13%)
  local copies, waits for them, and re-layouts  9.19 us (9%)
  other arithmetic  1.04 us (1%)
    all_to_all x3, waiting for transfers between devices, exchange(): return lax.all_to_all(x, 'kvp', 0, 0, tiled=True)  29.9 us
    all_to_all x3, starting transfers between devices, exchange(): return lax.all_to_all(x, 'kvp', 0, 0, tiled=True)  15.8 us
    all_to_all x1, blocking collectives, exchange(): return lax.all_to_all(x, 'kvp', 0, 0, tiled=True)  14 us
    ppermute x5, starting transfers between devices, swap(): return lax.ppermute(x, 'tp', [(i, i ^ bits) for i in range(devices)])  9.12 us
    unnamed x18, local copies, waits for them, and re-layouts  8.37 us
    ppermute x5, waiting for transfers between devices, swap(): return lax.ppermute(x, 'tp', [(i, i ^ bits) for i in range(devices)])  7.49 us
    pallas_call x1, Pallas kernels, local(): pl.pallas_call(functools.partial(attention_kernel, scaling, batch), out_s...  7.45 us
    pallas_call x1, Pallas kernels, local(): pl.pallas_call(project_kernel, out_shape=jax.ShapeDtypeStruct((owners, ro...  2.76 us
  transfers between devices with their start and end apart: 8, of which 7 were waited for; matrix products, arithmetic and copies ran while one was open for 1% of the time, Pallas kernels for 0%

profile of v2, /device:TPU:1, one launch (start us, length us, event | category | flops | bytes accessed | tf_op | source)
XLA Modules:
  0.0 99.2 jit_solution(14063685502069796329)
XLA Ops:
  0.0 0.0 copy-start.2
  0.0 1.2 %copy-done.2 = bf16[512,1024]{1,0:T(8,128)(2,1)S(1)} copy-done((bf16[512,1024]{1,0:T(8,128)(2,1)S(1)}, bf16[512,1024]{1,0:T(8,128)(2,1)}, u32[]{:S(2)}) %copy-start.2) | copy-done | bytes 1048600
  1.2 0.0 copy-start.4
  1.2 0.9 copy-done.4
  2.2 0.0 copy-start.5
  2.2 0.9 copy-done.5
  3.1 0.0 copy-start.6
  3.1 0.9 copy-done.6
  4.0 0.0 copy-start.7
  4.0 0.0 copy-start.8
  4.0 2.8 %shard_map.100 = bf16[16,16,1280]{2,1,0:T(8,128)(2,1)} custom-call(bf16[2,128,512]{2,1,0:T(8,128)(2,1)S(1)} %copy-done.4, bf16[512,1024]{1,0:T(8,128)(2,1)S(1)} %copy-done.2, bf16[512,128]{1,0:T(8,128)(2,1)S(1)} %copy-done.5, bf16[512,128]{1,0:T(8,128)(2,1)S(1)} %copy-done.6), custom_call_target="tpu_custom_call" | custom-call | tf_op jit(solution)/shard_map/pallas_call | solution.py:318
  6.8 8.6 %all-to-all-start = ((bf16[16,16,1280]{2,1,0:T(8,128)(2,1)}), bf16[16,16,1280]{2,1,0:T(8,128)(2,1)S(1)}, u32[]{:S(2)}, u32[]{:S(2)}) async-start(bf16[16,16,1280]{2,1,0:T(8,128)(2,1)} %shard_map.100), calls=%async_computation | async-start | bytes 1310720 | tf_op jit(solution)/shard_map/all_to_all | solution.py:314
  15.4 0.7 dynamic_slice.3
  16.1 0.1 convert_element_type.32
  16.2 0.1 fusion
  16.4 0.1 pad_maximum_fusion
  16.4 10.7 %all-to-all-done.parts_ref = bf16[16,16,1280]{2,1,0:T(8,128)(2,1)S(1)} async-done(((bf16[16,16,1280]{2,1,0:T(8,128)(2,1)}), bf16[16,16,1280]{2,1,0:T(8,128)(2,1)S(1)}, u32[]{:S(2)}, u32[]{:S(2)}) %all-to-all-start) | async-done | bytes 655392 | tf_op jit(solution)/shard_map/all_to_all | solution.py:314
  27.2 0.2 shard_map.101
  27.3 14.0 %all_to_all.20 = bf16[16,128,128]{2,1,0:T(8,128)(2,1)S(1)} all-to-all(bf16[16,128,128]{2,1,0:T(8,128)(2,1)S(1)} %get-tuple-element.9), channel_id=1, replica_groups=mesh['kvp'=16,'tp'=8] {'kvp'}, dimensions={0} | all-to-all | bytes 1048576 | tf_op jit(solution)/shard_map/all_to_all | solution.py:314
  41.3 0.0 copy-done.7
  41.3 0.0 copy-done.8
  41.3 0.0 copy-start
  41.3 2.2 %copy-done = bf16[64,256,128]{2,1,0:T(8,128)(2,1)S(1)} copy-done((bf16[64,256,128]{2,1,0:T(8,128)(2,1)S(1)}, bf16[64,256,128]{2,1,0:T(8,128)(2,1)}, u32[]{:S(2)}) %copy-start) | copy-done | bytes 4194328
  43.5 0.0 copy-start.1
  43.5 2.2 %copy-done.1 = bf16[64,256,128]{2,1,0:T(8,128)(2,1)S(1)} copy-done((bf16[64,256,128]{2,1,0:T(8,128)(2,1)S(1)}, bf16[64,256,128]{2,1,0:T(8,128)(2,1)}, u32[]{:S(2)}) %copy-start.1) | copy-done | bytes 4194328
  45.7 0.0 copy-start.3
  45.7 7.5 %shard_map.102 = bf16[16,144,128]{2,1,0:T(8,128)(2,1)} custom-call(s32[64]{0:T(128)S(1)} %copy-done.7, s32[64]{0:T(128)S(1)} %copy-done.8, bf16[128,16,128]{2,1,0:T(8,128)(2,1)S(1)} %bitcast.6, bf16[64,256,128]{2,1,0:T(8,128)(2,1)S(1)} %copy-done, bf16[64,256,128]{2,1,0:T(8,128)(2,1)S(1)} %copy-done.1), custom_call_target="tpu_custom_call" | custom-call | tf_op jit(solution)/shard_map/pallas_call | solution.py:347
  53.2 3.6 %all-to-all-start.2 = ((bf16[16,144,128]{2,1,0:T(8,128)(2,1)}), bf16[16,144,128]{2,1,0:T(8,128)(2,1)S(1)}, u32[]{:S(2)}, u32[]{:S(2)}) async-start(bf16[16,144,128]{2,1,0:T(8,128)(2,1)} %shard_map.102), calls=%async_computation.2 | async-start | bytes 1179648 | tf_op jit(solution)/shard_map/all_to_all | solution.py:314
  56.8 10.3 %all-to-all-done.2.parts_ref = bf16[16,144,128]{2,1,0:T(8,128)(2,1)S(1)} async-done(((bf16[16,144,128]{2,1,0:T(8,128)(2,1)}), bf16[16,144,128]{2,1,0:T(8,128)(2,1)S(1)}, u32[]{:S(2)}, u32[]{:S(2)}) %all-to-all-start.2) | async-done | bytes 589856 | tf_op jit(solution)/shard_map/all_to_all | solution.py:314
  67.0 1.7 %shard_map.103 = bf16[16,16,1024]{2,1,0:T(8,128)(2,1)} custom-call(bf16[16,144,128]{2,1,0:T(8,128)(2,1)S(1)} %all-to-all-done.2.parts_ref, bf16[128,128]{1,0:T(8,128)(2,1)S(1)} %slice_bitcast_fusion.q_ref, bf16[2,16,128]{2,1,0:T(8,128)(2,1)S(1)} %get-tuple-element.10.new_ref), custom_call_target="tpu_custom_call" | custom-call | tf_op jit(solution)/shard_map/pallas_call | solution.py:358
  68.7 3.6 %all-to-all-start.3 = ((bf16[16,16,1024]{2,1,0:T(8,128)(2,1)}), bf16[16,16,1024]{2,1,0:T(8,128)(2,1)S(1)}, u32[]{:S(2)}, u32[]{:S(2)}) async-start(bf16[16,16,1024]{2,1,0:T(8,128)(2,1)} %shard_map.103), calls=%async_computation.3 | async-start | bytes 1048576 | tf_op jit(solution)/shard_map/all_to_all | solution.py:314
  72.3 8.9 %all-to-all-done.3.heads_ref = bf16[16,16,1024]{2,1,0:T(8,128)(2,1)S(1)} async-done(((bf16[16,16,1024]{2,1,0:T(8,128)(2,1)}), bf16[16,16,1024]{2,1,0:T(8,128)(2,1)S(1)}, u32[]{:S(2)}, u32[]{:S(2)}) %all-to-all-start.3) | async-done | bytes 524320 | tf_op jit(solution)/shard_map/all_to_all | solution.py:314
  81.3 0.0 copy-done.3
  81.3 0.4 shard_map.104
  81.7 4.2 %collective-permute-start = (bf16[128,512]{1,0:T(8,128)(2,1)S(1)}, bf16[128,512]{1,0:T(8,128)(2,1)S(1)}, u32[]{:S(2)}, u32[]{:S(2)}) collective-permute-start(bf16[128,512]{1,0:T(8,128)(2,1)S(1)} %get-tuple-element.12), channel_id=1, source_target_pairs={{0,1},{1,0},{2,3},{3,2},{4,5},{5,4},{6,7},{7,6},{8,9},{9,8},{10,11... | collective-permute-start | bytes 393224 | tf_op jit(solution)/shard_map/ppermute | solution.py:382
  85.9 1.0 collective-permute-done
  86.9 2.8 %collective-permute-start.3 = (bf16[128,512]{1,0:T(8,128)(2,1)S(1)}, bf16[128,512]{1,0:T(8,128)(2,1)S(1)}, u32[]{:S(2)}, u32[]{:S(2)}) collective-permute-start(bf16[128,512]{1,0:T(8,128)(2,1)S(1)} %add_convert_fusion.1), channel_id=1, source_target_pairs={{0,4},{1,5},{2,6},{3,7},{4,0},{5,1},{6,2},{7,3},{8,12},{9,13},{10,... | collective-permute-start | bytes 393224 | tf_op jit(solution)/shard_map/ppermute | solution.py:382
  89.7 0.9 collective-permute-start.2
  90.6 0.0 collective-permute-start.1
  90.6 2.6 %collective-permute-done.3 = bf16[128,512]{1,0:T(8,128)(2,1)S(1)} collective-permute-done((bf16[128,512]{1,0:T(8,128)(2,1)S(1)}, bf16[128,512]{1,0:T(8,128)(2,1)S(1)}, u32[]{:S(2)}, u32[]{:S(2)}) %collective-permute-start.3) | collective-permute-done | bytes 131104 | tf_op jit(solution)/shard_map/ppermute | solution.py:382
  93.2 2.9 %collective-permute-done.2 = bf16[128,512]{1,0:T(8,128)(2,1)S(1)} collective-permute-done((bf16[128,512]{1,0:T(8,128)(2,1)S(1)}, bf16[128,512]{1,0:T(8,128)(2,1)S(1)}, u32[]{:S(2)}, u32[]{:S(2)}) %collective-permute-start.2) | collective-permute-done | bytes 131104 | tf_op jit(solution)/shard_map/ppermute | solution.py:382
  96.1 0.0 collective-permute-done.1
  96.1 0.1 add_convert_fusion
  96.2 1.3 %collective-permute-start.4 = (bf16[128,512]{1,0:T(8,128)(2,1)S(1)}, bf16[128,512]{1,0:T(8,128)(2,1)S(1)}, u32[]{:S(2)}, u32[]{:S(2)}) collective-permute-start(bf16[128,512]{1,0:T(8,128)(2,1)S(1)} %add_convert_fusion), channel_id=1, source_target_pairs={{0,1},{1,0},{2,3},{3,2},{4,5},{5,4},{6,7},{7,6},{8,9},{9,8},{10,11... | collective-permute-start | bytes 393224 | tf_op jit(solution)/shard_map/ppermute | solution.py:382
  97.4 1.0 collective-permute-done.4
  98.4 0.7 maximum_select_fusion
  (4 shorter events, 0.0 us)
Async XLA Ops:
  0.0 1.2 %copy-start.2 = (bf16[512,1024]{1,0:T(8,128)(2,1)S(1)}, bf16[512,1024]{1,0:T(8,128)(2,1)}, u32[]{:S(2)}) copy-start(bf16[512,1024]{1,0:T(8,128)(2,1)} %wq_hbm.1) | copy-start | bytes 3145732
  1.2 0.9 copy-start.4
  2.2 0.9 copy-start.5
  3.1 0.9 copy-start.6
  4.0 37.3 %copy-start.7 = (s32[64]{0:T(128)S(1)}, s32[64]{0:T(128)}, u32[]{:S(2)}) copy-start(s32[64]{0:T(128)} %request_ref.1) | copy-start | bytes 772
  4.0 37.3 %copy-start.8 = (s32[64]{0:T(128)S(1)}, s32[64]{0:T(128)}, u32[]{:S(2)}) copy-start(s32[64]{0:T(128)} %fill_ref.1) | copy-start | bytes 772
  6.8 20.4 %all-to-all-start = ((bf16[16,16,1280]{2,1,0:T(8,128)(2,1)}), bf16[16,16,1280]{2,1,0:T(8,128)(2,1)S(1)}, u32[]{:S(2)}, u32[]{:S(2)}) async-start(bf16[16,16,1280]{2,1,0:T(8,128)(2,1)} %shard_map.100), calls=%async_computation | async-start | bytes 1310720 | tf_op jit(solution)/shard_map/all_to_all | solution.py:314
  41.3 2.2 %copy-start = (bf16[64,256,128]{2,1,0:T(8,128)(2,1)S(1)}, bf16[64,256,128]{2,1,0:T(8,128)(2,1)}, u32[]{:S(2)}) copy-start(bf16[64,256,128]{2,1,0:T(8,128)(2,1)} %k_hbm.1) | copy-start | bytes 12582916
  43.5 2.2 %copy-start.1 = (bf16[64,256,128]{2,1,0:T(8,128)(2,1)S(1)}, bf16[64,256,128]{2,1,0:T(8,128)(2,1)}, u32[]{:S(2)}) copy-start(bf16[64,256,128]{2,1,0:T(8,128)(2,1)} %v_hbm.1) | copy-start | bytes 12582916
  45.7 35.6 %copy-start.3 = (bf16[1024,512]{1,0:T(8,128)(2,1)S(1)}, bf16[1024,512]{1,0:T(8,128)(2,1)}, u32[]{:S(2)}) copy-start(bf16[1024,512]{1,0:T(8,128)(2,1)} %w_ref.1) | copy-start | bytes 3145732
  53.2 13.9 %all-to-all-start.2 = ((bf16[16,144,128]{2,1,0:T(8,128)(2,1)}), bf16[16,144,128]{2,1,0:T(8,128)(2,1)S(1)}, u32[]{:S(2)}, u32[]{:S(2)}) async-start(bf16[16,144,128]{2,1,0:T(8,128)(2,1)} %shard_map.102), calls=%async_computation.2 | async-start | bytes 1179648 | tf_op jit(solution)/shard_map/all_to_all | solution.py:314
  68.7 12.5 %all-to-all-start.3 = ((bf16[16,16,1024]{2,1,0:T(8,128)(2,1)}), bf16[16,16,1024]{2,1,0:T(8,128)(2,1)S(1)}, u32[]{:S(2)}, u32[]{:S(2)}) async-start(bf16[16,16,1024]{2,1,0:T(8,128)(2,1)} %shard_map.103), calls=%async_computation.3 | async-start | bytes 1048576 | tf_op jit(solution)/shard_map/all_to_all | solution.py:314
  81.7 5.2 %collective-permute-start = (bf16[128,512]{1,0:T(8,128)(2,1)S(1)}, bf16[128,512]{1,0:T(8,128)(2,1)S(1)}, u32[]{:S(2)}, u32[]{:S(2)}) collective-permute-start(bf16[128,512]{1,0:T(8,128)(2,1)S(1)} %get-tuple-element.12), channel_id=1, source_target_pairs={{0,1},{1,0},{2,3},{3,2},{4,5},{5,4},{6,7},{7,6},{8,9},{9,8},{10,11... | collective-permute-start | bytes 393224 | tf_op jit(solution)/shard_map/ppermute | solution.py:382
  86.9 6.3 %collective-permute-start.3 = (bf16[128,512]{1,0:T(8,128)(2,1)S(1)}, bf16[128,512]{1,0:T(8,128)(2,1)S(1)}, u32[]{:S(2)}, u32[]{:S(2)}) collective-permute-start(bf16[128,512]{1,0:T(8,128)(2,1)S(1)} %add_convert_fusion.1), channel_id=1, source_target_pairs={{0,4},{1,5},{2,6},{3,7},{4,0},{5,1},{6,2},{7,3},{8,12},{9,13},{10,... | collective-permute-start | bytes 393224 | tf_op jit(solution)/shard_map/ppermute | solution.py:382
  89.7 6.3 %collective-permute-start.2 = (bf16[128,512]{1,0:T(8,128)(2,1)S(1)}, bf16[128,512]{1,0:T(8,128)(2,1)S(1)}, u32[]{:S(2)}, u32[]{:S(2)}) collective-permute-start(bf16[128,512]{1,0:T(8,128)(2,1)S(1)} %add_convert_fusion.1), channel_id=1, source_target_pairs={{0,6},{1,7},{2,4},{3,5},{4,2},{5,3},{6,0},{7,1},{8,14},{9,15},{10,... | collective-permute-start | bytes 393224 | tf_op jit(solution)/shard_map/ppermute | solution.py:382
  90.6 5.5 %collective-permute-start.1 = (bf16[128,512]{1,0:T(8,128)(2,1)S(1)}, bf16[128,512]{1,0:T(8,128)(2,1)S(1)}, u32[]{:S(2)}, u32[]{:S(2)}) collective-permute-start(bf16[128,512]{1,0:T(8,128)(2,1)S(1)} %add_convert_fusion.1), channel_id=1, source_target_pairs={{0,2},{1,3},{2,0},{3,1},{4,6},{5,7},{6,4},{7,5},{8,10},{9,11},{10,... | collective-permute-start | bytes 393224 | tf_op jit(solution)/shard_map/ppermute | solution.py:382
  96.2 2.3 %collective-permute-start.4 = (bf16[128,512]{1,0:T(8,128)(2,1)S(1)}, bf16[128,512]{1,0:T(8,128)(2,1)S(1)}, u32[]{:S(2)}, u32[]{:S(2)}) collective-permute-start(bf16[128,512]{1,0:T(8,128)(2,1)S(1)} %add_convert_fusion), channel_id=1, source_target_pairs={{0,1},{1,0},{2,3},{3,2},{4,5},{5,4},{6,7},{7,6},{8,9},{9,8},{10,11... | collective-permute-start | bytes 393224 | tf_op jit(solution)/shard_map/ppermute | solution.py:382

commit v3 on v2

--- a/solution.py
+++ b/solution.py
@@ -21,6 +21,10 @@
 
 def params(mib=24):
     return pltpu.CompilerParams(vmem_limit_bytes=mib * 1024 * 1024)
+
+
+def in_hbm(*arrays):
+    return [pltpu.with_memory_space_constraint(a, pltpu.HBM) for a in arrays]
 
 
 def rotation_tables(positions, first, count, steps):
@@ -326,7 +330,7 @@
             pltpu.SemaphoreType.DMA((group + 3,)),
         ],
         compiler_params=params(),
-    )(hidden_in, w_query, key_weight_matrix, value_weight_matrix)
+    )(*in_hbm(hidden_in, w_query, key_weight_matrix, value_weight_matrix))
     parts = exchange(parts)
     queries, new_rows = pl.pallas_call(
         rotate_kernel,
@@ -353,7 +357,7 @@
         + [pltpu.VMEM(sums, f32)] * 3
         + [pltpu.SemaphoreType.DMA((2, blocks // batch))],
         compiler_params=params(32),
-    )(block_request, block_fill, queries, paged_key_cache, paged_value_cache)
+    )(block_request, block_fill, queries, *in_hbm(paged_key_cache, paged_value_cache))
     parts = exchange(parts)
     heads = pl.pallas_call(
         functools.partial(finish_kernel, scaling),

time: 99.8 us -> 92.5 us (0.927)
  local copies, waits for them, and re-layouts: 9.19 us -> 0.83 us
  Pallas kernels: 12.5 us -> 13.8 us
    unnamed x18 -> x6, local copies, waits for them, and re-layouts: 8.37 us -> 0.01 us
  transfers between devices with their start and end apart: 8 -> 8, of which waited for: 7 -> 8; matrix products, arithmetic and copies ran while one was open for 1% -> 1% of each run, Pallas kernels for 0% -> 0%
where the time goes in v3:
time: 92.5 us; the launch traced here: 92 us
  waiting for transfers between devices  37.4 us (40%)
  starting transfers between devices  24.9 us (27%)
  blocking collectives  14 us (15%)
  Pallas kernels  13.8 us (15%)
  other arithmetic  1.04 us (1%)
    all_to_all x3, waiting for transfers between devices, exchange(): return lax.all_to_all(x, 'kvp', 0, 0, tiled=True)  29.9 us
    all_to_all x3, starting transfers between devices, exchange(): return lax.all_to_all(x, 'kvp', 0, 0, tiled=True)  15.8 us
    all_to_all x1, blocking collectives, exchange(): return lax.all_to_all(x, 'kvp', 0, 0, tiled=True)  14 us
    ppermute x5, starting transfers between devices, swap(): return lax.ppermute(x, 'tp', [(i, i ^ bits) for i in range(devices)])  9.1 us
    pallas_call x1, Pallas kernels, local(): pl.pallas_call(functools.partial(attention_kernel, scaling, batch), out_s...  7.88 us
    ppermute x5, waiting for transfers between devices, swap(): return lax.ppermute(x, 'tp', [(i, i ^ bits) for i in range(devices)])  7.51 us
    pallas_call x1, Pallas kernels, local(): pl.pallas_call(project_kernel, out_shape=jax.ShapeDtypeStruct((owners, ro...  3.57 us
  transfers between devices with their start and end apart: 8, of which 8 were waited for; matrix products, arithmetic and copies ran while one was open for 1% of the time, Pallas kernels for 0%

profile of v3, /device:TPU:1, one launch (start us, length us, event | category | flops | bytes accessed | tf_op | source)
XLA Modules:
  0.0 92.0 jit_solution(5341204899637827999)
XLA Ops:
  0.0 0.0 copy-start.2
  0.0 0.0 copy-start.1
  0.0 3.6 %shard_map.100 = bf16[16,16,1280]{2,1,0:T(8,128)(2,1)} custom-call(bf16[2,128,512]{2,1,0:T(8,128)(2,1)} %hidden_hbm.1, bf16[512,1024]{1,0:T(8,128)(2,1)} %wq_hbm.1, bf16[512,128]{1,0:T(8,128)(2,1)} %wk_hbm.1, bf16[512,128]{1,0:T(8,128)(2,1)} %wv_hbm.1), custom_call_target="tpu_custom_call" | custom-call | tf_op jit(solution)/shard_map/pallas_call | solution.py:322
  3.6 8.6 %all-to-all-start = ((bf16[16,16,1280]{2,1,0:T(8,128)(2,1)}), bf16[16,16,1280]{2,1,0:T(8,128)(2,1)S(1)}, u32[]{:S(2)}, u32[]{:S(2)}) async-start(bf16[16,16,1280]{2,1,0:T(8,128)(2,1)} %shard_map.100), calls=%async_computation | async-start | bytes 1310720 | tf_op jit(solution)/shard_map/all_to_all | solution.py:318
  12.2 0.7 dynamic_slice.3
  13.0 0.1 convert_element_type.32
  13.0 0.1 fusion
  13.2 0.1 pad_maximum_fusion
  13.3 10.7 %all-to-all-done.parts_ref = bf16[16,16,1280]{2,1,0:T(8,128)(2,1)S(1)} async-done(((bf16[16,16,1280]{2,1,0:T(8,128)(2,1)}), bf16[16,16,1280]{2,1,0:T(8,128)(2,1)S(1)}, u32[]{:S(2)}, u32[]{:S(2)}) %all-to-all-start) | async-done | bytes 655392 | tf_op jit(solution)/shard_map/all_to_all | solution.py:318
  24.0 0.2 shard_map.101
  24.2 14.0 %all_to_all.20 = bf16[16,128,128]{2,1,0:T(8,128)(2,1)S(1)} all-to-all(bf16[16,128,128]{2,1,0:T(8,128)(2,1)S(1)} %get-tuple-element.9), channel_id=1, replica_groups=mesh['kvp'=16,'tp'=8] {'kvp'}, dimensions={0} | all-to-all | bytes 1048576 | tf_op jit(solution)/shard_map/all_to_all | solution.py:318
  38.2 0.0 copy-done.2
  38.2 0.0 copy-done.1
  38.2 0.0 copy-start
  38.2 7.9 %shard_map.102 = bf16[16,144,128]{2,1,0:T(8,128)(2,1)} custom-call(s32[64]{0:T(128)S(1)} %copy-done.1, s32[64]{0:T(128)S(1)} %copy-done.2, bf16[128,16,128]{2,1,0:T(8,128)(2,1)S(1)} %bitcast.6, bf16[64,256,128]{2,1,0:T(8,128)(2,1)} %k_hbm.1, bf16[64,256,128]{2,1,0:T(8,128)(2,1)} %v_hbm.1), custom_call_target="tpu_custom_call" | custom-call | tf_op jit(solution)/shard_map/pallas_call | solution.py:351
  46.1 3.6 %all-to-all-start.2 = ((bf16[16,144,128]{2,1,0:T(8,128)(2,1)}), bf16[16,144,128]{2,1,0:T(8,128)(2,1)S(1)}, u32[]{:S(2)}, u32[]{:S(2)}) async-start(bf16[16,144,128]{2,1,0:T(8,128)(2,1)} %shard_map.102), calls=%async_computation.2 | async-start | bytes 1179648 | tf_op jit(solution)/shard_map/all_to_all | solution.py:318
  49.7 10.2 %all-to-all-done.2.parts_ref = bf16[16,144,128]{2,1,0:T(8,128)(2,1)S(1)} async-done(((bf16[16,144,128]{2,1,0:T(8,128)(2,1)}), bf16[16,144,128]{2,1,0:T(8,128)(2,1)S(1)}, u32[]{:S(2)}, u32[]{:S(2)}) %all-to-all-start.2) | async-done | bytes 589856 | tf_op jit(solution)/shard_map/all_to_all | solution.py:318
  59.9 1.7 %shard_map.103 = bf16[16,16,1024]{2,1,0:T(8,128)(2,1)} custom-call(bf16[16,144,128]{2,1,0:T(8,128)(2,1)S(1)} %all-to-all-done.2.parts_ref, bf16[128,128]{1,0:T(8,128)(2,1)S(1)} %slice_bitcast_fusion.q_ref, bf16[2,16,128]{2,1,0:T(8,128)(2,1)S(1)} %get-tuple-element.10.new_ref), custom_call_target="tpu_custom_call" | custom-call | tf_op jit(solution)/shard_map/pallas_call | solution.py:362
  61.6 3.6 %all-to-all-start.3 = ((bf16[16,16,1024]{2,1,0:T(8,128)(2,1)}), bf16[16,16,1024]{2,1,0:T(8,128)(2,1)S(1)}, u32[]{:S(2)}, u32[]{:S(2)}) async-start(bf16[16,16,1024]{2,1,0:T(8,128)(2,1)} %shard_map.103), calls=%async_computation.3 | async-start | bytes 1048576 | tf_op jit(solution)/shard_map/all_to_all | solution.py:318
  65.2 8.9 %all-to-all-done.3.heads_ref = bf16[16,16,1024]{2,1,0:T(8,128)(2,1)S(1)} async-done(((bf16[16,16,1024]{2,1,0:T(8,128)(2,1)}), bf16[16,16,1024]{2,1,0:T(8,128)(2,1)S(1)}, u32[]{:S(2)}, u32[]{:S(2)}) %all-to-all-start.3) | async-done | bytes 524320 | tf_op jit(solution)/shard_map/all_to_all | solution.py:318
  74.1 0.0 copy-done
  74.1 0.4 shard_map.104
  74.6 4.2 %collective-permute-start = (bf16[128,512]{1,0:T(8,128)(2,1)S(1)}, bf16[128,512]{1,0:T(8,128)(2,1)S(1)}, u32[]{:S(2)}, u32[]{:S(2)}) collective-permute-start(bf16[128,512]{1,0:T(8,128)(2,1)S(1)} %get-tuple-element.12), channel_id=1, source_target_pairs={{0,1},{1,0},{2,3},{3,2},{4,5},{5,4},{6,7},{7,6},{8,9},{9,8},{10,11... | collective-permute-start | bytes 393224 | tf_op jit(solution)/shard_map/ppermute | solution.py:386
  78.8 1.0 %collective-permute-done = bf16[128,512]{1,0:T(8,128)(2,1)S(1)} collective-permute-done((bf16[128,512]{1,0:T(8,128)(2,1)S(1)}, bf16[128,512]{1,0:T(8,128)(2,1)S(1)}, u32[]{:S(2)}, u32[]{:S(2)}) %collective-permute-start) | collective-permute-done | bytes 131104 | tf_op jit(solution)/shard_map/ppermute | solution.py:386
  79.8 2.8 %collective-permute-start.3 = (bf16[128,512]{1,0:T(8,128)(2,1)S(1)}, bf16[128,512]{1,0:T(8,128)(2,1)S(1)}, u32[]{:S(2)}, u32[]{:S(2)}) collective-permute-start(bf16[128,512]{1,0:T(8,128)(2,1)S(1)} %add_convert_fusion.1), channel_id=1, source_target_pairs={{0,4},{1,5},{2,6},{3,7},{4,0},{5,1},{6,2},{7,3},{8,12},{9,13},{10,... | collective-permute-start | bytes 393224 | tf_op jit(solution)/shard_map/ppermute | solution.py:386
  82.6 0.9 collective-permute-start.2
  83.5 0.0 collective-permute-start.1
  83.5 2.6 %collective-permute-done.3 = bf16[128,512]{1,0:T(8,128)(2,1)S(1)} collective-permute-done((bf16[128,512]{1,0:T(8,128)(2,1)S(1)}, bf16[128,512]{1,0:T(8,128)(2,1)S(1)}, u32[]{:S(2)}, u32[]{:S(2)}) %collective-permute-start.3) | collective-permute-done | bytes 131104 | tf_op jit(solution)/shard_map/ppermute | solution.py:386
  86.1 2.9 %collective-permute-done.2 = bf16[128,512]{1,0:T(8,128)(2,1)S(1)} collective-permute-done((bf16[128,512]{1,0:T(8,128)(2,1)S(1)}, bf16[128,512]{1,0:T(8,128)(2,1)S(1)}, u32[]{:S(2)}, u32[]{:S(2)}) %collective-permute-start.2) | collective-permute-done | bytes 131104 | tf_op jit(solution)/shard_map/ppermute | solution.py:386
  88.9 0.1 collective-permute-done.1
  89.0 0.1 add_convert_fusion
  89.1 1.2 %collective-permute-start.4 = (bf16[128,512]{1,0:T(8,128)(2,1)S(1)}, bf16[128,512]{1,0:T(8,128)(2,1)S(1)}, u32[]{:S(2)}, u32[]{:S(2)}) collective-permute-start(bf16[128,512]{1,0:T(8,128)(2,1)S(1)} %add_convert_fusion), channel_id=1, source_target_pairs={{0,1},{1,0},{2,3},{3,2},{4,5},{5,4},{6,7},{7,6},{8,9},{9,8},{10,11... | collective-permute-start | bytes 393224 | tf_op jit(solution)/shard_map/ppermute | solution.py:386
  90.3 1.0 %collective-permute-done.4 = bf16[128,512]{1,0:T(8,128)(2,1)S(1)} collective-permute-done((bf16[128,512]{1,0:T(8,128)(2,1)S(1)}, bf16[128,512]{1,0:T(8,128)(2,1)S(1)}, u32[]{:S(2)}, u32[]{:S(2)}) %collective-permute-start.4) | collective-permute-done | bytes 131104 | tf_op jit(solution)/shard_map/ppermute | solution.py:386
  91.3 0.7 maximum_select_fusion
  (4 shorter events, 0.0 us)
Async XLA Ops:
  0.0 38.2 %copy-start.2 = (s32[64]{0:T(128)S(1)}, s32[64]{0:T(128)}, u32[]{:S(2)}) copy-start(s32[64]{0:T(128)} %fill_ref.1) | copy-start | bytes 772
  0.0 38.2 %copy-start.1 = (s32[64]{0:T(128)S(1)}, s32[64]{0:T(128)}, u32[]{:S(2)}) copy-start(s32[64]{0:T(128)} %request_ref.1) | copy-start | bytes 772
  3.6 20.4 %all-to-all-start = ((bf16[16,16,1280]{2,1,0:T(8,128)(2,1)}), bf16[16,16,1280]{2,1,0:T(8,128)(2,1)S(1)}, u32[]{:S(2)}, u32[]{:S(2)}) async-start(bf16[16,16,1280]{2,1,0:T(8,128)(2,1)} %shard_map.100), calls=%async_computation | async-start | bytes 1310720 | tf_op jit(solution)/shard_map/all_to_all | solution.py:318
  38.2 36.0 %copy-start = (bf16[1024,512]{1,0:T(8,128)(2,1)S(1)}, bf16[1024,512]{1,0:T(8,128)(2,1)}, u32[]{:S(2)}) copy-start(bf16[1024,512]{1,0:T(8,128)(2,1)} %w_ref.1) | copy-start | bytes 3145732
  46.1 13.9 %all-to-all-start.2 = ((bf16[16,144,128]{2,1,0:T(8,128)(2,1)}), bf16[16,144,128]{2,1,0:T(8,128)(2,1)S(1)}, u32[]{:S(2)}, u32[]{:S(2)}) async-start(bf16[16,144,128]{2,1,0:T(8,128)(2,1)} %shard_map.102), calls=%async_computation.2 | async-start | bytes 1179648 | tf_op jit(solution)/shard_map/all_to_all | solution.py:318
  61.6 12.5 %all-to-all-start.3 = ((bf16[16,16,1024]{2,1,0:T(8,128)(2,1)}), bf16[16,16,1024]{2,1,0:T(8,128)(2,1)S(1)}, u32[]{:S(2)}, u32[]{:S(2)}) async-start(bf16[16,16,1024]{2,1,0:T(8,128)(2,1)} %shard_map.103), calls=%async_computation.3 | async-start | bytes 1048576 | tf_op jit(solution)/shard_map/all_to_all | solution.py:318
  74.6 5.2 %collective-permute-start = (bf16[128,512]{1,0:T(8,128)(2,1)S(1)}, bf16[128,512]{1,0:T(8,128)(2,1)S(1)}, u32[]{:S(2)}, u32[]{:S(2)}) collective-permute-start(bf16[128,512]{1,0:T(8,128)(2,1)S(1)} %get-tuple-element.12), channel_id=1, source_target_pairs={{0,1},{1,0},{2,3},{3,2},{4,5},{5,4},{6,7},{7,6},{8,9},{9,8},{10,11... | collective-permute-start | bytes 393224 | tf_op jit(solution)/shard_map/ppermute | solution.py:386
  79.8 6.3 %collective-permute-start.3 = (bf16[128,512]{1,0:T(8,128)(2,1)S(1)}, bf16[128,512]{1,0:T(8,128)(2,1)S(1)}, u32[]{:S(2)}, u32[]{:S(2)}) collective-permute-start(bf16[128,512]{1,0:T(8,128)(2,1)S(1)} %add_convert_fusion.1), channel_id=1, source_target_pairs={{0,4},{1,5},{2,6},{3,7},{4,0},{5,1},{6,2},{7,3},{8,12},{9,13},{10,... | collective-permute-start | bytes 393224 | tf_op jit(solution)/shard_map/ppermute | solution.py:386
  82.6 6.3 %collective-permute-start.2 = (bf16[128,512]{1,0:T(8,128)(2,1)S(1)}, bf16[128,512]{1,0:T(8,128)(2,1)S(1)}, u32[]{:S(2)}, u32[]{:S(2)}) collective-permute-start(bf16[128,512]{1,0:T(8,128)(2,1)S(1)} %add_convert_fusion.1), channel_id=1, source_target_pairs={{0,6},{1,7},{2,4},{3,5},{4,2},{5,3},{6,0},{7,1},{8,14},{9,15},{10,... | collective-permute-start | bytes 393224 | tf_op jit(solution)/shard_map/ppermute | solution.py:386
  83.5 5.5 %collective-permute-start.1 = (bf16[128,512]{1,0:T(8,128)(2,1)S(1)}, bf16[128,512]{1,0:T(8,128)(2,1)S(1)}, u32[]{:S(2)}, u32[]{:S(2)}) collective-permute-start(bf16[128,512]{1,0:T(8,128)(2,1)S(1)} %add_convert_fusion.1), channel_id=1, source_target_pairs={{0,2},{1,3},{2,0},{3,1},{4,6},{5,7},{6,4},{7,5},{8,10},{9,11},{10,... | collective-permute-start | bytes 393224 | tf_op jit(solution)/shard_map/ppermute | solution.py:386
  89.1 2.2 %collective-permute-start.4 = (bf16[128,512]{1,0:T(8,128)(2,1)S(1)}, bf16[128,512]{1,0:T(8,128)(2,1)S(1)}, u32[]{:S(2)}, u32[]{:S(2)}) collective-permute-start(bf16[128,512]{1,0:T(8,128)(2,1)S(1)} %add_convert_fusion), channel_id=1, source_target_pairs={{0,1},{1,0},{2,3},{3,2},{4,5},{5,4},{6,7},{7,6},{8,9},{9,8},{10,11... | collective-permute-start | bytes 393224 | tf_op jit(solution)/shard_map/ppermute | solution.py:386

commit v4 on v3

--- a/solution.py
+++ b/solution.py
@@ -27,12 +27,10 @@
     return [pltpu.with_memory_space_constraint(a, pltpu.HBM) for a in arrays]
 
 
-def rotation_tables(positions, first, count, steps):
+def rotation_tables(slots):
     half = HEAD_SIZE // 2
     inverse = rope_base ** (-(jnp.arange(half, dtype=jnp.float32) * 2.0 / HEAD_SIZE))
-    own = lax.dynamic_slice_in_dim(positions, first, count)
-    slots = own[None, :] + jnp.arange(steps, dtype=jnp.int32)[:, None]
-    angles = slots.reshape(-1).astype(jnp.float32)[:, None] * inverse
+    angles = slots[:, :half] * inverse
     cosine, sine = jnp.cos(angles), jnp.sin(angles)
     return (
         jnp.concatenate([cosine, cosine], axis=-1),
@@ -40,39 +38,60 @@
     )
 
 
-def project_kernel(hidden_hbm, wq_hbm, wk_hbm, wv_hbm, out_ref, hidden_ref, w_ref, sems):
+def project_kernel(
+    position_hbm,
+    hidden_hbm,
+    wq_hbm,
+    wk_hbm,
+    wv_hbm,
+    out_ref,
+    slot_ref,
+    position_ref,
+    hidden_ref,
+    wq_ref,
+    wk_ref,
+    wv_ref,
+    sems,
+):
     steps, requests, width = hidden_ref.shape
     owners, rows, columns = out_ref.shape
     own = rows // steps
-    copies = [pltpu.make_async_copy(hidden_hbm, hidden_ref, sems.at[0])]
-    chunks = []
-    column = 0
-    for hbm in (wq_hbm, wk_hbm, wv_hbm):
-        total = hbm.shape[1]
+    sources = (position_hbm, hidden_hbm, wk_hbm, wv_hbm, wq_hbm)
+    targets = (position_ref, hidden_ref, wk_ref, wv_ref, wq_ref)
+    copies = [
+        pltpu.make_async_copy(source, target, sems.at[i])
+        for i, (source, target) in enumerate(zip(sources, targets))
+    ]
+    for copy in copies:
+        copy.start()
+    first = lax.axis_index("kvp") * own
+    copies[0].wait()
+    row = lax.broadcasted_iota(jnp.int32, (rows, HEAD_SIZE), 0)
+    slots = jnp.zeros((rows, HEAD_SIZE), jnp.int32)
+    for r in range(own):
+        slots = jnp.where(row % own == r, position_ref[first + r], slots)
+    slot_ref[...] = (slots + row // own).astype(jnp.float32)
+    copies[1].wait()
+    hidden = hidden_ref[...].reshape(steps * requests, width)
+    queries = wq_ref.shape[1]
+    starts = (queries, queries + wk_ref.shape[1], 0)
+    for copy, ref, column in zip(copies[2:], targets[2:], starts):
+        copy.wait()
+        total = ref.shape[1]
         chunk = min(total, 256)
         for start in range(0, total, chunk):
-            lanes = slice(column, column + chunk)
-            copies.append(
-                pltpu.make_async_copy(
-                    hbm.at[:, start : start + chunk], w_ref.at[:, lanes], sems.at[len(copies)]
-                )
+            part = jnp.dot(
+                hidden, ref[:, start : start + chunk], preferred_element_type=jnp.float32
             )
-            chunks.append(lanes)
-            column += chunk
-    for copy in copies:
-        copy.start()
-    copies[0].wait()
-    hidden = hidden_ref[...].reshape(steps * requests, width)
-    for copy, lanes in zip(copies[1:], chunks):
-        copy.wait()
-        part = jnp.dot(hidden, w_ref[:, lanes], preferred_element_type=jnp.float32)
-        split = [
-            part[s * requests : (s + 1) * requests].reshape(owners, own, -1) for s in range(steps)
-        ]
-        out_ref[:, :, lanes] = jnp.concatenate(split, axis=1).astype(jnp.bfloat16)
-
-
-def rotate_kernel(parts_ref, cos_ref, sin_ref, q_ref, new_ref, turned_ref):
+            split = [
+                part[s * requests : (s + 1) * requests].reshape(owners, own, chunk)
+                for s in range(steps)
+            ]
+            lanes = slice(column + start, column + start + chunk)
+            out_ref[:, :, lanes] = jnp.concatenate(split, axis=1).astype(jnp.bfloat16)
+
+
+def rotate_kernel(parts_ref, cos_ref, sin_ref, q_ref, own_ref, new_ref, turned_ref):
     sources, rows, columns = parts_ref.shape
     steps = 2
     own = rows // steps
@@ -95,6 +114,7 @@
     new_ref[0] = rope(head(group)).astype(jnp.bfloat16)
     new_ref[1] = head(group + 1).astype(jnp.bfloat16)
     queries = turned_ref[...].astype(jnp.bfloat16)
+    own_ref[...] = queries
     for d in range(q_ref.shape[0]):
         q_ref[d] = queries
 
@@ -140,75 +160,92 @@
     total_ref[...] = jnp.zeros_like(total_ref)
     sum_ref[...] = jnp.zeros_like(sum_ref)
 
-    slot = lax.broadcasted_iota(jnp.int32, (slots, lanes), 0)
-    lane_block = lax.broadcasted_iota(jnp.int32, (1, lanes), 1) // rows
-    empty = jnp.zeros((rows, HEAD_SIZE), jnp.bfloat16)
-
-    def group_step(g, _):
+    slot = lax.broadcasted_iota(jnp.int32, (lanes, slots), 1)
+
+    def score(g):
         first = g * batch
-        owners = [request_ref[first + b] for b in range(batch)]
-
-        def placed(b):
-            return jnp.concatenate(
-                [empty] * b + [q_ref[owners[b]]] + [empty] * (batch - b - 1), axis=0
-            )
-
         load(k_hbm, k_ref, 0, g).wait()
-        scores = jnp.zeros((slots, lanes), jnp.float32)
-        for b in range(0, batch, 2):
-            scores = scores + lax.dot_general(
-                jnp.concatenate([k_ref[first + b], k_ref[first + b + 1]], axis=1),
-                jnp.concatenate([placed(b), placed(b + 1)], axis=1),
-                NT,
+        return jnp.concatenate(
+            [
+                lax.dot_general(
+                    q_ref[request_ref[first + b]],
+                    k_ref[first + b],
+                    NT,
+                    preferred_element_type=jnp.float32,
+                )
+                for b in range(batch)
+            ],
+            axis=0,
+        )
+
+    def weigh(g, scores):
+        first = g * batch
+        fill = jnp.concatenate(
+            [jnp.full((rows, 1), fill_ref[first + b], jnp.int32) for b in range(batch)], axis=0
+        )
+        scores = jnp.where(slot < fill, scores * scaling, floor_score)
+        largest = jnp.max(scores, axis=1, keepdims=True)
+        weights = jnp.exp(scores - largest).astype(jnp.bfloat16)
+        total = jnp.sum(weights.astype(jnp.float32), axis=1, keepdims=True)
+        load(v_hbm, v_ref, 1, g).wait()
+        summed = [
+            jnp.dot(
+                weights[b * rows : (b + 1) * rows],
+                v_ref[first + b],
                 preferred_element_type=jnp.float32,
             )
-        fill = jnp.zeros((1, lanes), jnp.int32)
-        for b in range(batch):
-            fill = jnp.where(lane_block == b, fill_ref[first + b], fill)
-        scores = jnp.where(slot < fill, scores * scaling, floor_score)
-        largest = jnp.max(scores, axis=0, keepdims=True)
-        weights = jnp.exp(scores - largest).astype(jnp.bfloat16).astype(jnp.float32)
-        total = jnp.sum(weights, axis=0, keepdims=True)
-        turned = weights.T.astype(jnp.bfloat16)
-        stats = jnp.concatenate(
-            [largest, total, jnp.zeros((6, lanes), jnp.float32)], axis=0
-        ).T
-        load(v_hbm, v_ref, 1, g).wait()
+            for b in range(batch)
+        ]
+        return largest, total, summed
+
+    def merge(g, largest, total, summed):
         for b in range(batch):
             mine = slice(b * rows, (b + 1) * rows)
-            summed = jnp.dot(turned[mine], v_ref[first + b], preferred_element_type=jnp.float32)
-            owner = owners[b]
+            owner = request_ref[g * batch + b]
             before = max_ref[owner]
-            block_max = stats[mine, 0:1]
-            after = jnp.maximum(before, block_max)
+            after = jnp.maximum(before, largest[mine])
             keep = jnp.exp(before - after)
-            add = jnp.exp(block_max - after)
+            add = jnp.exp(largest[mine] - after)
             max_ref[owner] = after
-            total_ref[owner] = total_ref[owner] * keep + stats[mine, 1:2] * add
-            sum_ref[owner] = sum_ref[owner] * keep + summed * add
-        return 0
-
-    lax.fori_loop(0, groups, group_step, 0)
+            total_ref[owner] = total_ref[owner] * keep + total[mine] * add
+            sum_ref[owner] = sum_ref[owner] * keep + summed[b] * add
+
+    scores = score(0)
+    for g in range(groups):
+        later = score(g + 1) if g + 1 < groups else None
+        merge(g, *weigh(g, scores))
+        scores = later
 
     owners = out_ref.shape[0]
     own = requests // owners
     flat = own * rows
-    lane = lax.broadcasted_iota(jnp.int32, (flat, HEAD_SIZE), 1)
-    pick = (
-        lax.broadcasted_iota(jnp.int32, (STAT_ROWS, HEAD_SIZE), 0)
-        == lax.broadcasted_iota(jnp.int32, (STAT_ROWS, HEAD_SIZE), 1)
-    ).astype(jnp.bfloat16)
+    diagonal = lax.broadcasted_iota(jnp.int32, (flat, HEAD_SIZE), 0) == lax.broadcasted_iota(
+        jnp.int32, (flat, HEAD_SIZE), 1
+    )
+
+    def by_lane(ref):
+        return jnp.concatenate(
+            [
+                jnp.sum(
+                    jnp.where(
+                        diagonal, ref[d * own : (d + 1) * own].reshape(flat, HEAD_SIZE), 0.0
+                    ),
+                    axis=0,
+                    keepdims=True,
+                )
+                for d in range(owners)
+            ],
+            axis=0,
+        )
+
+    values = pieces(by_lane(max_ref)) + pieces(by_lane(total_ref))
+    empty = jnp.zeros((STAT_ROWS - len(values), HEAD_SIZE), jnp.float32)
     for d in range(owners):
-        mine = slice(d * own, (d + 1) * own)
-        out_ref[d, :flat, :] = sum_ref[mine].reshape(flat, HEAD_SIZE).astype(jnp.bfloat16)
-        values = pieces(max_ref[mine].reshape(flat, HEAD_SIZE)) + pieces(
-            total_ref[mine].reshape(flat, HEAD_SIZE)
-        )
-        table = jnp.zeros((flat, HEAD_SIZE), jnp.float32)
-        for i, value in enumerate(values):
-            table = jnp.where(lane == i, value, table)
-        out_ref[d, flat:, :] = lax.dot_general(
-            pick, table.astype(jnp.bfloat16), NT, preferred_element_type=jnp.float32
+        out_ref[d, :flat, :] = (
+            sum_ref[d * own : (d + 1) * own].reshape(flat, HEAD_SIZE).astype(jnp.bfloat16)
+        )
+        out_ref[d, flat:, :] = jnp.concatenate(
+            [value[d : d + 1] for value in values] + [empty], axis=0
         ).astype(jnp.bfloat16)
 
 
@@ -317,33 +354,43 @@
     def exchange(x):
         return lax.all_to_all(x, "kvp", 0, 0, tiled=True)
 
-    cosine, sine = rotation_tables(positions, lax.axis_index("kvp") * own, own, steps)
+    tp = lax.axis_index("tp")
+    core = tp % 2
+    hidden_in, core = lax.optimization_barrier((hidden_in, core))
     columns = (group + 2) * HEAD_SIZE
-    parts = pl.pallas_call(
+    parts, row_slots = pl.pallas_call(
         project_kernel,
-        out_shape=jax.ShapeDtypeStruct((owners, rows, columns), bf16),
-        in_specs=[HBM] * 4,
-        out_specs=VMEM,
+        out_shape=(
+            jax.ShapeDtypeStruct((owners, rows, columns), bf16),
+            jax.ShapeDtypeStruct((rows, HEAD_SIZE), f32),
+        ),
+        in_specs=[HBM] * 5,
+        out_specs=(VMEM, VMEM),
         scratch_shapes=[
+            pltpu.SMEM(positions.shape, jnp.int32),
             pltpu.VMEM(hidden_in.shape, bf16),
-            pltpu.VMEM((hidden_in.shape[2], columns), bf16),
-            pltpu.SemaphoreType.DMA((group + 3,)),
+            pltpu.VMEM(w_query.shape, bf16),
+            pltpu.VMEM(key_weight_matrix.shape, bf16),
+            pltpu.VMEM(value_weight_matrix.shape, bf16),
+            pltpu.SemaphoreType.DMA((5,)),
         ],
         compiler_params=params(),
-    )(*in_hbm(hidden_in, w_query, key_weight_matrix, value_weight_matrix))
+    )(*in_hbm(positions, hidden_in, w_query, key_weight_matrix, value_weight_matrix))
+    cosine, sine = rotation_tables(row_slots)
+    parts, cosine, sine = lax.optimization_barrier((parts, cosine, sine))
     parts = exchange(parts)
-    queries, new_rows = pl.pallas_call(
+    queries, own_queries, new_rows = pl.pallas_call(
         rotate_kernel,
         out_shape=(
             jax.ShapeDtypeStruct((owners, flat, HEAD_SIZE), bf16),
+            jax.ShapeDtypeStruct((flat, HEAD_SIZE), bf16),
             jax.ShapeDtypeStruct((2, rows, HEAD_SIZE), bf16),
         ),
         in_specs=[VMEM] * 3,
-        out_specs=(VMEM, VMEM),
+        out_specs=(VMEM, VMEM, VMEM),
         scratch_shapes=[pltpu.VMEM((flat, HEAD_SIZE), f32)],
         compiler_params=params(),
     )(parts, cosine, sine)
-    own_queries = queries[0]
     queries = exchange(queries).reshape(requests, steps * group, HEAD_SIZE)
 
     batch = 16
@@ -369,8 +416,6 @@
     )(parts, own_queries, new_rows)
     heads = exchange(heads)
 
-    tp = lax.axis_index("tp")
-    core = tp % 2
     half = (owners * own, out_columns)
     keep, send = pl.pallas_call(
         output_kernel,

time: 92.5 us -> 84.6 us (0.915)
  blocking collectives: 14 us -> 56.6 us
  waiting for transfers between devices: 37.4 us -> 7.49 us
  starting transfers between devices: 24.9 us -> 10.8 us
  Pallas kernels: 13.8 us -> 8.38 us
    all_to_all x1 -> x4, blocking collectives: 14 us -> 56.6 us  [exchange(): return lax.all_to_all(x, 'kvp', 0, 0, tiled=True)]
    all_to_all x3 -> x0, waiting for transfers between devices: 29.9 us -> none  [exchange(): return lax.all_to_all(x, 'kvp', 0, 0, tiled=True)]
    all_to_all x3 -> x0, starting transfers between devices: 15.8 us -> none  [exchange(): return lax.all_to_all(x, 'kvp', 0, 0, tiled=True)]
    pallas_call x1, Pallas kernels: 7.88 us -> 4.93 us  [local(): pl.pallas_call(functools.partial(attention_kernel, scaling, batch), out_s...]
    ppermute x5, starting transfers between devices: 9.1 us -> 10.8 us  [swap(): return lax.ppermute(x, 'tp', [(i, i ^ bits) for i in range(devices)])]
    pallas_call x1, Pallas kernels: 3.57 us -> 1.93 us  [local(): pl.pallas_call(project_kernel, out_shape=(jax.ShapeDtypeStruct((owners, r...]
  transfers between devices with their start and end apart: 8 -> 5, of which waited for: 8 -> 4; matrix products, arithmetic and copies ran while one was open for 1% -> 0% of each run, Pallas kernels for 0% -> 0%
where the time goes in v4:
time: 84.6 us; the launch traced here: 84.4 us
  blocking collectives  56.6 us (67%)
  starting transfers between devices  10.8 us (13%)
  Pallas kernels  8.38 us (10%)
  waiting for transfers between devices  7.49 us (9%)
  other arithmetic  0.96 us (1%)
    all_to_all x4, blocking collectives, exchange(): return lax.all_to_all(x, 'kvp', 0, 0, tiled=True)  56.6 us
    ppermute x5, starting transfers between devices, swap(): return lax.ppermute(x, 'tp', [(i, i ^ bits) for i in range(devices)])  10.8 us
    ppermute x5, waiting for transfers between devices, swap(): return lax.ppermute(x, 'tp', [(i, i ^ bits) for i in range(devices)])  7.49 us
    pallas_call x1, Pallas kernels, local(): pl.pallas_call(functools.partial(attention_kernel, scaling, batch), out_s...  4.93 us
    pallas_call x1, Pallas kernels, local(): pl.pallas_call(project_kernel, out_shape=(jax.ShapeDtypeStruct((owners, r...  1.93 us
  transfers between devices with their start and end apart: 5, of which 4 were waited for; matrix products, arithmetic and copies ran while one was open for 0% of the time, Pallas kernels for 0%

profile of v4, /device:TPU:1, one launch (start us, length us, event | category | flops | bytes accessed | tf_op | source)
XLA Modules:
  0.0 84.4 jit_solution(8079725686660628834)
XLA Ops:
  0.0 0.0 copy-start.1
  0.0 0.0 copy-start.2
  0.0 1.9 %shard_map.100 = (bf16[16,16,1280]{2,1,0:T(8,128)(2,1)S(1)}, f32[16,128]{1,0:T(8,128)S(1)}) custom-call(s32[128]{0:T(128)} %position_hbm.1, bf16[2,128,512]{2,1,0:T(8,128)(2,1)} %hidden_hbm, bf16[512,1024]{1,0:T(8,128)(2,1)} %wq_hbm.1, bf16[512,128]{1,0:T(8,128)(2,1)} %wk_hbm.1, bf16[512,128]{1,0:T(8,128)(2,1)} %wv_hbm.1), custom_call_target="tpu_custom_call" | custom-call | tf_op jit(solution)/shard_map/pallas_call | solution.py:361
  2.0 0.1 fusion.2
  2.0 0.1 pad_maximum_fusion
  2.1 20.2 %all_to_all.20.parts_ref = bf16[16,16,1280]{2,1,0:T(8,128)(2,1)S(1)} all-to-all(bf16[16,16,1280]{2,1,0:T(8,128)(2,1)S(1)} %get-tuple-element.21), channel_id=1, replica_groups=mesh['kvp'=16,'tp'=8] {'kvp'}, dimensions={0} | all-to-all | bytes 1310720 | tf_op jit(solution)/shard_map/all_to_all | solution.py:355
  22.3 0.2 shard_map.101
  22.5 12.5 %all_to_all.21 = bf16[16,128,128]{2,1,0:T(8,128)(2,1)S(1)} all-to-all(bf16[16,128,128]{2,1,0:T(8,128)(2,1)S(1)} %get-tuple-element.24), channel_id=1, replica_groups=mesh['kvp'=16,'tp'=8] {'kvp'}, dimensions={0} | all-to-all | bytes 1048576 | tf_op jit(solution)/shard_map/all_to_all | solution.py:355
  35.0 0.0 copy-done.1
  35.0 0.0 copy-done.2
  35.0 0.0 copy-start
  35.0 4.9 %shard_map.102 = bf16[16,144,128]{2,1,0:T(8,128)(2,1)S(1)} custom-call(s32[64]{0:T(128)S(1)} %copy-done.1, s32[64]{0:T(128)S(1)} %copy-done.2, bf16[128,16,128]{2,1,0:T(8,128)(2,1)S(1)} %bitcast.4, bf16[64,256,128]{2,1,0:T(8,128)(2,1)} %k_hbm.1, bf16[64,256,128]{2,1,0:T(8,128)(2,1)} %v_hbm.1), custom_call_target="tpu_custom_call" | custom-call | tf_op jit(solution)/shard_map/pallas_call | solution.py:398
  39.9 11.9 %all_to_all.22.parts_ref = bf16[16,144,128]{2,1,0:T(8,128)(2,1)S(1)} all-to-all(bf16[16,144,128]{2,1,0:T(8,128)(2,1)S(1)} %shard_map.102), channel_id=1, replica_groups=mesh['kvp'=16,'tp'=8] {'kvp'}, dimensions={0} | all-to-all | bytes 1179648 | tf_op jit(solution)/shard_map/all_to_all | solution.py:355
  51.8 0.9 %shard_map.103 = bf16[16,16,1024]{2,1,0:T(8,128)(2,1)S(1)} custom-call(bf16[16,144,128]{2,1,0:T(8,128)(2,1)S(1)} %all_to_all.22.parts_ref, bf16[128,128]{1,0:T(8,128)(2,1)S(1)} %get-tuple-element.25.q_ref, bf16[2,16,128]{2,1,0:T(8,128)(2,1)S(1)} %get-tuple-element.26.new_ref), custom_call_target="tpu_custom_call" | custom-call | tf_op jit(solution)/shard_map/pallas_call | solution.py:409
  52.7 12.0 %all_to_all.23.heads_ref = bf16[16,16,1024]{2,1,0:T(8,128)(2,1)S(1)} all-to-all(bf16[16,16,1024]{2,1,0:T(8,128)(2,1)S(1)} %shard_map.103), channel_id=1, replica_groups=mesh['kvp'=16,'tp'=8] {'kvp'}, dimensions={0} | all-to-all | bytes 1048576 | tf_op jit(solution)/shard_map/all_to_all | solution.py:355
  64.8 0.0 copy-done
  64.8 0.4 shard_map.104
  65.2 5.9 %collective-permute-start = (bf16[128,512]{1,0:T(8,128)(2,1)S(1)}, bf16[128,512]{1,0:T(8,128)(2,1)S(1)}, u32[]{:S(2)}, u32[]{:S(2)}) collective-permute-start(bf16[128,512]{1,0:T(8,128)(2,1)S(1)} %get-tuple-element.28), channel_id=1, source_target_pairs={{0,1},{1,0},{2,3},{3,2},{4,5},{5,4},{6,7},{7,6},{8,9},{9,8},{10,11... | collective-permute-start | bytes 393224 | tf_op jit(solution)/shard_map/ppermute | solution.py:431
  71.1 1.0 %collective-permute-done = bf16[128,512]{1,0:T(8,128)(2,1)S(1)} collective-permute-done((bf16[128,512]{1,0:T(8,128)(2,1)S(1)}, bf16[128,512]{1,0:T(8,128)(2,1)S(1)}, u32[]{:S(2)}, u32[]{:S(2)}) %collective-permute-start) | collective-permute-done | bytes 131104 | tf_op jit(solution)/shard_map/ppermute | solution.py:431
  72.1 2.8 %collective-permute-start.3 = (bf16[128,512]{1,0:T(8,128)(2,1)S(1)}, bf16[128,512]{1,0:T(8,128)(2,1)S(1)}, u32[]{:S(2)}, u32[]{:S(2)}) collective-permute-start(bf16[128,512]{1,0:T(8,128)(2,1)S(1)} %add_convert_fusion.1), channel_id=1, source_target_pairs={{0,4},{1,5},{2,6},{3,7},{4,0},{5,1},{6,2},{7,3},{8,12},{9,13},{10,... | collective-permute-start | bytes 393224 | tf_op jit(solution)/shard_map/ppermute | solution.py:431
  74.9 0.9 %collective-permute-start.2 = (bf16[128,512]{1,0:T(8,128)(2,1)S(1)}, bf16[128,512]{1,0:T(8,128)(2,1)S(1)}, u32[]{:S(2)}, u32[]{:S(2)}) collective-permute-start(bf16[128,512]{1,0:T(8,128)(2,1)S(1)} %add_convert_fusion.1), channel_id=1, source_target_pairs={{0,6},{1,7},{2,4},{3,5},{4,2},{5,3},{6,0},{7,1},{8,14},{9,15},{10,... | collective-permute-start | bytes 393224 | tf_op jit(solution)/shard_map/ppermute | solution.py:431
  75.8 0.0 collective-permute-start.1
  75.8 2.6 %collective-permute-done.3 = bf16[128,512]{1,0:T(8,128)(2,1)S(1)} collective-permute-done((bf16[128,512]{1,0:T(8,128)(2,1)S(1)}, bf16[128,512]{1,0:T(8,128)(2,1)S(1)}, u32[]{:S(2)}, u32[]{:S(2)}) %collective-permute-start.3) | collective-permute-done | bytes 131104 | tf_op jit(solution)/shard_map/ppermute | solution.py:431
  78.4 2.8 %collective-permute-done.2 = bf16[128,512]{1,0:T(8,128)(2,1)S(1)} collective-permute-done((bf16[128,512]{1,0:T(8,128)(2,1)S(1)}, bf16[128,512]{1,0:T(8,128)(2,1)S(1)}, u32[]{:S(2)}, u32[]{:S(2)}) %collective-permute-start.2) | collective-permute-done | bytes 131104 | tf_op jit(solution)/shard_map/ppermute | solution.py:431
  81.3 0.0 collective-permute-done.1
  81.3 0.1 add_convert_fusion
  81.4 1.3 %collective-permute-start.4 = (bf16[128,512]{1,0:T(8,128)(2,1)S(1)}, bf16[128,512]{1,0:T(8,128)(2,1)S(1)}, u32[]{:S(2)}, u32[]{:S(2)}) collective-permute-start(bf16[128,512]{1,0:T(8,128)(2,1)S(1)} %add_convert_fusion), channel_id=1, source_target_pairs={{0,1},{1,0},{2,3},{3,2},{4,5},{5,4},{6,7},{7,6},{8,9},{9,8},{10,11... | collective-permute-start | bytes 393224 | tf_op jit(solution)/shard_map/ppermute | solution.py:431
  82.7 1.0 %collective-permute-done.4 = bf16[128,512]{1,0:T(8,128)(2,1)S(1)} collective-permute-done((bf16[128,512]{1,0:T(8,128)(2,1)S(1)}, bf16[128,512]{1,0:T(8,128)(2,1)S(1)}, u32[]{:S(2)}, u32[]{:S(2)}) %collective-permute-start.4) | collective-permute-done | bytes 131104 | tf_op jit(solution)/shard_map/ppermute | solution.py:431
  83.6 0.7 maximum_select_fusion
  (2 shorter events, 0.0 us)
Async XLA Ops:
  0.0 35.0 %copy-start.1 = (s32[64]{0:T(128)S(1)}, s32[64]{0:T(128)}, u32[]{:S(2)}) copy-start(s32[64]{0:T(128)} %request_ref.1) | copy-start | bytes 772
  0.0 35.0 %copy-start.2 = (s32[64]{0:T(128)S(1)}, s32[64]{0:T(128)}, u32[]{:S(2)}) copy-start(s32[64]{0:T(128)} %fill_ref.1) | copy-start | bytes 772
  35.0 29.8 %copy-start = (bf16[1024,512]{1,0:T(8,128)(2,1)S(1)}, bf16[1024,512]{1,0:T(8,128)(2,1)}, u32[]{:S(2)}) copy-start(bf16[1024,512]{1,0:T(8,128)(2,1)} %w_ref.1) | copy-start | bytes 3145732
  65.2 6.9 %collective-permute-start = (bf16[128,512]{1,0:T(8,128)(2,1)S(1)}, bf16[128,512]{1,0:T(8,128)(2,1)S(1)}, u32[]{:S(2)}, u32[]{:S(2)}) collective-permute-start(bf16[128,512]{1,0:T(8,128)(2,1)S(1)} %get-tuple-element.28), channel_id=1, source_target_pairs={{0,1},{1,0},{2,3},{3,2},{4,5},{5,4},{6,7},{7,6},{8,9},{9,8},{10,11... | collective-permute-start | bytes 393224 | tf_op jit(solution)/shard_map/ppermute | solution.py:431
  72.1 6.3 %collective-permute-start.3 = (bf16[128,512]{1,0:T(8,128)(2,1)S(1)}, bf16[128,512]{1,0:T(8,128)(2,1)S(1)}, u32[]{:S(2)}, u32[]{:S(2)}) collective-permute-start(bf16[128,512]{1,0:T(8,128)(2,1)S(1)} %add_convert_fusion.1), channel_id=1, source_target_pairs={{0,4},{1,5},{2,6},{3,7},{4,0},{5,1},{6,2},{7,3},{8,12},{9,13},{10,... | collective-permute-start | bytes 393224 | tf_op jit(solution)/shard_map/ppermute | solution.py:431
  74.9 6.3 %collective-permute-start.2 = (bf16[128,512]{1,0:T(8,128)(2,1)S(1)}, bf16[128,512]{1,0:T(8,128)(2,1)S(1)}, u32[]{:S(2)}, u32[]{:S(2)}) collective-permute-start(bf16[128,512]{1,0:T(8,128)(2,1)S(1)} %add_convert_fusion.1), channel_id=1, source_target_pairs={{0,6},{1,7},{2,4},{3,5},{4,2},{5,3},{6,0},{7,1},{8,14},{9,15},{10,... | collective-permute-start | bytes 393224 | tf_op jit(solution)/shard_map/ppermute | solution.py:431
  75.8 5.5 %collective-permute-start.1 = (bf16[128,512]{1,0:T(8,128)(2,1)S(1)}, bf16[128,512]{1,0:T(8,128)(2,1)S(1)}, u32[]{:S(2)}, u32[]{:S(2)}) collective-permute-start(bf16[128,512]{1,0:T(8,128)(2,1)S(1)} %add_convert_fusion.1), channel_id=1, source_target_pairs={{0,2},{1,3},{2,0},{3,1},{4,6},{5,7},{6,4},{7,5},{8,10},{9,11},{10,... | collective-permute-start | bytes 393224 | tf_op jit(solution)/shard_map/ppermute | solution.py:431
  81.4 2.3 %collective-permute-start.4 = (bf16[128,512]{1,0:T(8,128)(2,1)S(1)}, bf16[128,512]{1,0:T(8,128)(2,1)S(1)}, u32[]{:S(2)}, u32[]{:S(2)}) collective-permute-start(bf16[128,512]{1,0:T(8,128)(2,1)S(1)} %add_convert_fusion), channel_id=1, source_target_pairs={{0,1},{1,0},{2,3},{3,2},{4,5},{5,4},{6,7},{7,6},{8,9},{9,8},{10,11... | collective-permute-start | bytes 393224 | tf_op jit(solution)/shard_map/ppermute | solution.py:431

commit v5 on v4

--- a/solution.py
+++ b/solution.py
@@ -25,6 +25,10 @@
 
 def in_hbm(*arrays):
     return [pltpu.with_memory_space_constraint(a, pltpu.HBM) for a in arrays]
+
+
+def in_vmem(*arrays):
+    return [pltpu.with_memory_space_constraint(a, pltpu.VMEM) for a in arrays]
 
 
 def rotation_tables(slots):
@@ -91,7 +95,7 @@
             out_ref[:, :, lanes] = jnp.concatenate(split, axis=1).astype(jnp.bfloat16)
 
 
-def rotate_kernel(parts_ref, cos_ref, sin_ref, q_ref, own_ref, new_ref, turned_ref):
+def rotate_kernel(parts_ref, cos_ref, sin_ref, keys_hbm, values_hbm, q_ref, own_ref, new_ref, turned_ref):
     sources, rows, columns = parts_ref.shape
     steps = 2
     own = rows // steps
@@ -134,28 +138,18 @@
     request_ref,
     fill_ref,
     q_ref,
-    k_hbm,
-    v_hbm,
-    out_ref,
     k_ref,
     v_ref,
+    out_ref,
     max_ref,
     total_ref,
     sum_ref,
-    sems,
 ):
     blocks, slots, _ = k_ref.shape
     requests, rows, _ = q_ref.shape
     groups = blocks // batch
     lanes = batch * rows
 
-    def load(hbm, ref, which, g):
-        span = pl.ds(g * batch, batch)
-        return pltpu.make_async_copy(hbm.at[span], ref.at[span], sems.at[which, g])
-
-    for g in range(groups):
-        load(k_hbm, k_ref, 0, g).start()
-        load(v_hbm, v_ref, 1, g).start()
     max_ref[...] = jnp.full_like(max_ref, floor_score)
     total_ref[...] = jnp.zeros_like(total_ref)
     sum_ref[...] = jnp.zeros_like(sum_ref)
@@ -164,7 +158,6 @@
 
     def score(g):
         first = g * batch
-        load(k_hbm, k_ref, 0, g).wait()
         return jnp.concatenate(
             [
                 lax.dot_general(
@@ -187,7 +180,6 @@
         largest = jnp.max(scores, axis=1, keepdims=True)
         weights = jnp.exp(scores - largest).astype(jnp.bfloat16)
         total = jnp.sum(weights.astype(jnp.float32), axis=1, keepdims=True)
-        load(v_hbm, v_ref, 1, g).wait()
         summed = [
             jnp.dot(
                 weights[b * rows : (b + 1) * rows],
@@ -386,11 +378,11 @@
             jax.ShapeDtypeStruct((flat, HEAD_SIZE), bf16),
             jax.ShapeDtypeStruct((2, rows, HEAD_SIZE), bf16),
         ),
-        in_specs=[VMEM] * 3,
+        in_specs=[VMEM] * 3 + [HBM] * 2,
         out_specs=(VMEM, VMEM, VMEM),
         scratch_shapes=[pltpu.VMEM((flat, HEAD_SIZE), f32)],
         compiler_params=params(),
-    )(parts, cosine, sine)
+    )(parts, cosine, sine, *in_hbm(paged_key_cache, paged_value_cache))
     queries = exchange(queries).reshape(requests, steps * group, HEAD_SIZE)
 
     batch = 16
@@ -398,13 +390,16 @@
     parts = pl.pallas_call(
         functools.partial(attention_kernel, scaling, batch),
         out_shape=jax.ShapeDtypeStruct((owners, flat + STAT_ROWS, HEAD_SIZE), bf16),
-        in_specs=[SMEM, SMEM, VMEM, HBM, HBM],
+        in_specs=[SMEM, SMEM, VMEM, VMEM, VMEM],
         out_specs=VMEM,
-        scratch_shapes=[pltpu.VMEM(paged_key_cache.shape, bf16)] * 2
-        + [pltpu.VMEM(sums, f32)] * 3
-        + [pltpu.SemaphoreType.DMA((2, blocks // batch))],
+        scratch_shapes=[pltpu.VMEM(sums, f32)] * 3,
         compiler_params=params(32),
-    )(block_request, block_fill, queries, *in_hbm(paged_key_cache, paged_value_cache))
+    )(
+        block_request,
+        block_fill,
+        queries,
+        *in_vmem(paged_key_cache, paged_value_cache),
+    )
     parts = exchange(parts)
     heads = pl.pallas_call(
         functools.partial(finish_kernel, scaling),

time: 84.6 us -> 82.6 us (0.976)
  Pallas kernels: 8.38 us -> 6.08 us
    pallas_call x1, Pallas kernels: 4.93 us -> 2.62 us  [local(): pl.pallas_call(functools.partial(attention_kernel, scaling, batch), out_s...]
  transfers between devices with their start and end apart: 5 -> 5, of which waited for: 4 -> 5; matrix products, arithmetic and copies ran while one was open for 0% -> 0% of each run, Pallas kernels for 0% -> 0%
where the time goes in v5:
time: 82.6 us; the launch traced here: 82.4 us
  blocking collectives  56.9 us (69%)
  starting transfers between devices  10.8 us (13%)
  waiting for transfers between devices  7.51 us (9%)
  Pallas kernels  6.08 us (7%)
  other arithmetic  0.96 us (1%)
    all_to_all x4, blocking collectives, exchange(): return lax.all_to_all(x, 'kvp', 0, 0, tiled=True)  56.9 us
    ppermute x5, starting transfers between devices, swap(): return lax.ppermute(x, 'tp', [(i, i ^ bits) for i in range(devices)])  10.8 us
    ppermute x5, waiting for transfers between devices, swap(): return lax.ppermute(x, 'tp', [(i, i ^ bits) for i in range(devices)])  7.51 us
    pallas_call x1, Pallas kernels, local(): pl.pallas_call(functools.partial(attention_kernel, scaling, batch), out_s...  2.62 us
    pallas_call x1, Pallas kernels, local(): pl.pallas_call(project_kernel, out_shape=(jax.ShapeDtypeStruct((owners, r...  1.93 us
  transfers between devices with their start and end apart: 5, of which 5 were waited for; matrix products, arithmetic and copies ran while one was open for 0% of the time, Pallas kernels for 0%

profile of v5, /device:TPU:1, one launch (start us, length us, event | category | flops | bytes accessed | tf_op | source)
XLA Modules:
  0.0 82.4 jit_solution(4094874297430873726)
XLA Ops:
  0.0 1.9 %shard_map.100 = (bf16[16,16,1280]{2,1,0:T(8,128)(2,1)S(1)}, f32[16,128]{1,0:T(8,128)S(1)}) custom-call(s32[128]{0:T(128)} %position_hbm.1, bf16[2,128,512]{2,1,0:T(8,128)(2,1)} %hidden_hbm, bf16[512,1024]{1,0:T(8,128)(2,1)} %wq_hbm.1, bf16[512,128]{1,0:T(8,128)(2,1)} %wk_hbm.1, bf16[512,128]{1,0:T(8,128)(2,1)} %wv_hbm.1), custom_call_target="tpu_custom_call" | custom-call | tf_op jit(solution)/shard_map/pallas_call | solution.py:353
  2.0 0.1 fusion.2
  2.0 0.1 pad_maximum_fusion
  2.1 20.2 %all_to_all.20.parts_ref = bf16[16,16,1280]{2,1,0:T(8,128)(2,1)S(1)} all-to-all(bf16[16,16,1280]{2,1,0:T(8,128)(2,1)S(1)} %get-tuple-element.21), channel_id=1, replica_groups=mesh['kvp'=16,'tp'=8] {'kvp'}, dimensions={0} | all-to-all | bytes 1310720 | tf_op jit(solution)/shard_map/all_to_all | solution.py:347
  22.3 0.0 copy-start
  22.3 0.0 copy-start.1
  22.3 0.0 copy-start.3
  22.3 0.0 copy-start.4
  22.3 0.2 shard_map.101
  22.5 12.7 %all_to_all.21 = bf16[16,128,128]{2,1,0:T(8,128)(2,1)S(1)} all-to-all(bf16[16,128,128]{2,1,0:T(8,128)(2,1)S(1)} %get-tuple-element.24), channel_id=1, replica_groups=mesh['kvp'=16,'tp'=8] {'kvp'}, dimensions={0} | all-to-all | bytes 1048576 | tf_op jit(solution)/shard_map/all_to_all | solution.py:347
  35.2 0.0 copy-done
  35.2 0.0 copy-done.1
  35.2 0.0 copy-done.3
  35.2 0.0 copy-done.4
  35.3 0.0 copy-start.2
  35.3 2.6 %shard_map.102 = bf16[16,144,128]{2,1,0:T(8,128)(2,1)S(1)} custom-call(s32[64]{0:T(128)S(1)} %copy-done.3, s32[64]{0:T(128)S(1)} %copy-done.4, bf16[128,16,128]{2,1,0:T(8,128)(2,1)S(1)} %bitcast.4, bf16[64,256,128]{2,1,0:T(8,128)(2,1)S(1)} %copy-done, bf16[64,256,128]{2,1,0:T(8,128)(2,1)S(1)} %copy-done.1), custom_call_target="tpu_custom_call" | custom-call | tf_op jit(solution)/shard_map/pallas_call | solution.py:390
  37.9 11.9 %all_to_all.22.parts_ref = bf16[16,144,128]{2,1,0:T(8,128)(2,1)S(1)} all-to-all(bf16[16,144,128]{2,1,0:T(8,128)(2,1)S(1)} %shard_map.102), channel_id=1, replica_groups=mesh['kvp'=16,'tp'=8] {'kvp'}, dimensions={0} | all-to-all | bytes 1179648 | tf_op jit(solution)/shard_map/all_to_all | solution.py:347
  49.8 0.9 %shard_map.103 = bf16[16,16,1024]{2,1,0:T(8,128)(2,1)S(1)} custom-call(bf16[16,144,128]{2,1,0:T(8,128)(2,1)S(1)} %all_to_all.22.parts_ref, bf16[128,128]{1,0:T(8,128)(2,1)S(1)} %get-tuple-element.25.q_ref, bf16[2,16,128]{2,1,0:T(8,128)(2,1)S(1)} %get-tuple-element.26.new_ref), custom_call_target="tpu_custom_call" | custom-call | tf_op jit(solution)/shard_map/pallas_call | solution.py:404
  50.7 12.0 %all_to_all.23.heads_ref = bf16[16,16,1024]{2,1,0:T(8,128)(2,1)S(1)} all-to-all(bf16[16,16,1024]{2,1,0:T(8,128)(2,1)S(1)} %shard_map.103), channel_id=1, replica_groups=mesh['kvp'=16,'tp'=8] {'kvp'}, dimensions={0} | all-to-all | bytes 1048576 | tf_op jit(solution)/shard_map/all_to_all | solution.py:347
  62.8 0.0 copy-done.2
  62.8 0.4 shard_map.104
  63.2 5.9 %collective-permute-start = (bf16[128,512]{1,0:T(8,128)(2,1)S(1)}, bf16[128,512]{1,0:T(8,128)(2,1)S(1)}, u32[]{:S(2)}, u32[]{:S(2)}) collective-permute-start(bf16[128,512]{1,0:T(8,128)(2,1)S(1)} %get-tuple-element.28), channel_id=1, source_target_pairs={{0,1},{1,0},{2,3},{3,2},{4,5},{5,4},{6,7},{7,6},{8,9},{9,8},{10,11... | collective-permute-start | bytes 393224 | tf_op jit(solution)/shard_map/ppermute | solution.py:426
  69.1 1.0 %collective-permute-done = bf16[128,512]{1,0:T(8,128)(2,1)S(1)} collective-permute-done((bf16[128,512]{1,0:T(8,128)(2,1)S(1)}, bf16[128,512]{1,0:T(8,128)(2,1)S(1)}, u32[]{:S(2)}, u32[]{:S(2)}) %collective-permute-start) | collective-permute-done | bytes 131104 | tf_op jit(solution)/shard_map/ppermute | solution.py:426
  70.1 2.8 %collective-permute-start.3 = (bf16[128,512]{1,0:T(8,128)(2,1)S(1)}, bf16[128,512]{1,0:T(8,128)(2,1)S(1)}, u32[]{:S(2)}, u32[]{:S(2)}) collective-permute-start(bf16[128,512]{1,0:T(8,128)(2,1)S(1)} %add_convert_fusion.1), channel_id=1, source_target_pairs={{0,4},{1,5},{2,6},{3,7},{4,0},{5,1},{6,2},{7,3},{8,12},{9,13},{10,... | collective-permute-start | bytes 393224 | tf_op jit(solution)/shard_map/ppermute | solution.py:426
  72.9 0.9 %collective-permute-start.2 = (bf16[128,512]{1,0:T(8,128)(2,1)S(1)}, bf16[128,512]{1,0:T(8,128)(2,1)S(1)}, u32[]{:S(2)}, u32[]{:S(2)}) collective-permute-start(bf16[128,512]{1,0:T(8,128)(2,1)S(1)} %add_convert_fusion.1), channel_id=1, source_target_pairs={{0,6},{1,7},{2,4},{3,5},{4,2},{5,3},{6,0},{7,1},{8,14},{9,15},{10,... | collective-permute-start | bytes 393224 | tf_op jit(solution)/shard_map/ppermute | solution.py:426
  73.8 0.0 collective-permute-start.1
  73.8 2.6 %collective-permute-done.3 = bf16[128,512]{1,0:T(8,128)(2,1)S(1)} collective-permute-done((bf16[128,512]{1,0:T(8,128)(2,1)S(1)}, bf16[128,512]{1,0:T(8,128)(2,1)S(1)}, u32[]{:S(2)}, u32[]{:S(2)}) %collective-permute-start.3) | collective-permute-done | bytes 131104 | tf_op jit(solution)/shard_map/ppermute | solution.py:426
  76.4 2.8 %collective-permute-done.2 = bf16[128,512]{1,0:T(8,128)(2,1)S(1)} collective-permute-done((bf16[128,512]{1,0:T(8,128)(2,1)S(1)}, bf16[128,512]{1,0:T(8,128)(2,1)S(1)}, u32[]{:S(2)}, u32[]{:S(2)}) %collective-permute-start.2) | collective-permute-done | bytes 131104 | tf_op jit(solution)/shard_map/ppermute | solution.py:426
  79.3 0.1 collective-permute-done.1
  79.3 0.1 add_convert_fusion
  79.4 1.2 %collective-permute-start.4 = (bf16[128,512]{1,0:T(8,128)(2,1)S(1)}, bf16[128,512]{1,0:T(8,128)(2,1)S(1)}, u32[]{:S(2)}, u32[]{:S(2)}) collective-permute-start(bf16[128,512]{1,0:T(8,128)(2,1)S(1)} %add_convert_fusion), channel_id=1, source_target_pairs={{0,1},{1,0},{2,3},{3,2},{4,5},{5,4},{6,7},{7,6},{8,9},{9,8},{10,11... | collective-permute-start | bytes 393224 | tf_op jit(solution)/shard_map/ppermute | solution.py:426
  80.6 1.0 %collective-permute-done.4 = bf16[128,512]{1,0:T(8,128)(2,1)S(1)} collective-permute-done((bf16[128,512]{1,0:T(8,128)(2,1)S(1)}, bf16[128,512]{1,0:T(8,128)(2,1)S(1)}, u32[]{:S(2)}, u32[]{:S(2)}) %collective-permute-start.4) | collective-permute-done | bytes 131104 | tf_op jit(solution)/shard_map/ppermute | solution.py:426
  81.6 0.7 maximum_select_fusion
  (2 shorter events, 0.0 us)
Async XLA Ops:
  22.3 13.0 %copy-start = (bf16[64,256,128]{2,1,0:T(8,128)(2,1)S(1)}, bf16[64,256,128]{2,1,0:T(8,128)(2,1)}, u32[]{:S(2)}) copy-start(bf16[64,256,128]{2,1,0:T(8,128)(2,1)} %k_ref.1) | copy-start | bytes 12582916
  22.3 13.0 %copy-start.1 = (bf16[64,256,128]{2,1,0:T(8,128)(2,1)S(1)}, bf16[64,256,128]{2,1,0:T(8,128)(2,1)}, u32[]{:S(2)}) copy-start(bf16[64,256,128]{2,1,0:T(8,128)(2,1)} %v_ref.1) | copy-start | bytes 12582916
  22.3 13.0 %copy-start.3 = (s32[64]{0:T(128)S(1)}, s32[64]{0:T(128)}, u32[]{:S(2)}) copy-start(s32[64]{0:T(128)} %request_ref.1) | copy-start | bytes 772
  22.3 13.0 %copy-start.4 = (s32[64]{0:T(128)S(1)}, s32[64]{0:T(128)}, u32[]{:S(2)}) copy-start(s32[64]{0:T(128)} %fill_ref.1) | copy-start | bytes 772
  35.3 27.5 %copy-start.2 = (bf16[1024,512]{1,0:T(8,128)(2,1)S(1)}, bf16[1024,512]{1,0:T(8,128)(2,1)}, u32[]{:S(2)}) copy-start(bf16[1024,512]{1,0:T(8,128)(2,1)} %w_ref.1) | copy-start | bytes 3145732
  63.2 6.9 %collective-permute-start = (bf16[128,512]{1,0:T(8,128)(2,1)S(1)}, bf16[128,512]{1,0:T(8,128)(2,1)S(1)}, u32[]{:S(2)}, u32[]{:S(2)}) collective-permute-start(bf16[128,512]{1,0:T(8,128)(2,1)S(1)} %get-tuple-element.28), channel_id=1, source_target_pairs={{0,1},{1,0},{2,3},{3,2},{4,5},{5,4},{6,7},{7,6},{8,9},{9,8},{10,11... | collective-permute-start | bytes 393224 | tf_op jit(solution)/shard_map/ppermute | solution.py:426
  70.1 6.3 %collective-permute-start.3 = (bf16[128,512]{1,0:T(8,128)(2,1)S(1)}, bf16[128,512]{1,0:T(8,128)(2,1)S(1)}, u32[]{:S(2)}, u32[]{:S(2)}) collective-permute-start(bf16[128,512]{1,0:T(8,128)(2,1)S(1)} %add_convert_fusion.1), channel_id=1, source_target_pairs={{0,4},{1,5},{2,6},{3,7},{4,0},{5,1},{6,2},{7,3},{8,12},{9,13},{10,... | collective-permute-start | bytes 393224 | tf_op jit(solution)/shard_map/ppermute | solution.py:426
  72.9 6.3 %collective-permute-start.2 = (bf16[128,512]{1,0:T(8,128)(2,1)S(1)}, bf16[128,512]{1,0:T(8,128)(2,1)S(1)}, u32[]{:S(2)}, u32[]{:S(2)}) collective-permute-start(bf16[128,512]{1,0:T(8,128)(2,1)S(1)} %add_convert_fusion.1), channel_id=1, source_target_pairs={{0,6},{1,7},{2,4},{3,5},{4,2},{5,3},{6,0},{7,1},{8,14},{9,15},{10,... | collective-permute-start | bytes 393224 | tf_op jit(solution)/shard_map/ppermute | solution.py:426
  73.8 5.5 %collective-permute-start.1 = (bf16[128,512]{1,0:T(8,128)(2,1)S(1)}, bf16[128,512]{1,0:T(8,128)(2,1)S(1)}, u32[]{:S(2)}, u32[]{:S(2)}) collective-permute-start(bf16[128,512]{1,0:T(8,128)(2,1)S(1)} %add_convert_fusion.1), channel_id=1, source_target_pairs={{0,2},{1,3},{2,0},{3,1},{4,6},{5,7},{6,4},{7,5},{8,10},{9,11},{10,... | collective-permute-start | bytes 393224 | tf_op jit(solution)/shard_map/ppermute | solution.py:426
  79.4 2.2 %collective-permute-start.4 = (bf16[128,512]{1,0:T(8,128)(2,1)S(1)}, bf16[128,512]{1,0:T(8,128)(2,1)S(1)}, u32[]{:S(2)}, u32[]{:S(2)}) collective-permute-start(bf16[128,512]{1,0:T(8,128)(2,1)S(1)} %add_convert_fusion), channel_id=1, source_target_pairs={{0,1},{1,0},{2,3},{3,2},{4,5},{5,4},{6,7},{7,6},{8,9},{9,8},{10,11... | collective-permute-start | bytes 393224 | tf_op jit(solution)/shard_map/ppermute | solution.py:426

commit v6 on v5

--- a/solution.py
+++ b/solution.py
@@ -33,13 +33,10 @@
 
 def rotation_tables(slots):
     half = HEAD_SIZE // 2
-    inverse = rope_base ** (-(jnp.arange(half, dtype=jnp.float32) * 2.0 / HEAD_SIZE))
-    angles = slots[:, :half] * inverse
-    cosine, sine = jnp.cos(angles), jnp.sin(angles)
-    return (
-        jnp.concatenate([cosine, cosine], axis=-1),
-        jnp.concatenate([-sine, sine], axis=-1),
-    )
+    pair = jnp.arange(HEAD_SIZE, dtype=jnp.int32) % half
+    inverse = rope_base ** (-(pair.astype(jnp.float32) * 2.0 / HEAD_SIZE))
+    angles = slots * inverse
+    return jnp.cos(angles), jnp.sin(angles)
 
 
 def project_kernel(
@@ -100,7 +97,9 @@
     steps = 2
     own = rows // steps
     group = columns // HEAD_SIZE - 2
-    cosine, sine = cos_ref[...], sin_ref[...]
+    lane = lax.broadcasted_iota(jnp.int32, (rows, HEAD_SIZE), 1)
+    cosine = cos_ref[...]
+    sine = jnp.where(lane < HEAD_SIZE // 2, -sin_ref[...], sin_ref[...])
 
     def head(index):
         lanes = slice(index * HEAD_SIZE, (index + 1) * HEAD_SIZE)
@@ -302,11 +301,10 @@
         out_ref[d] = heads
 
 
-def output_kernel(core_ref, heads_ref, w_ref, keep_ref, send_ref):
+def output_kernel(heads_ref, w_ref, out_ref):
     owners, rows, width = heads_ref.shape
-    steps = 2
+    steps = out_ref.shape[0]
     own = rows // steps
-    core = core_ref[0]
     heads = heads_ref[...].reshape(owners * rows, width)
     columns = w_ref.shape[1]
     chunk = min(columns, 256)
@@ -314,10 +312,10 @@
         lanes = slice(start, start + chunk)
         part = jnp.dot(heads, w_ref[:, lanes], preferred_element_type=jnp.float32)
         part = part.reshape(owners, rows, chunk)
-        first = part[:, :own].reshape(owners * own, chunk)
-        second = part[:, own:].reshape(owners * own, chunk)
-        keep_ref[:, lanes] = jnp.where(core == 0, first, second)
-        send_ref[:, lanes] = jnp.where(core == 0, second, first).astype(jnp.bfloat16)
+        for s in range(steps):
+            out_ref[s, :, lanes] = (
+                part[:, s * own : (s + 1) * own].reshape(owners * own, chunk).astype(jnp.bfloat16)
+            )
 
 
 def local(
@@ -346,9 +344,6 @@
     def exchange(x):
         return lax.all_to_all(x, "kvp", 0, 0, tiled=True)
 
-    tp = lax.axis_index("tp")
-    core = tp % 2
-    hidden_in, core = lax.optimization_barrier((hidden_in, core))
     columns = (group + 2) * HEAD_SIZE
     parts, row_slots = pl.pallas_call(
         project_kernel,
@@ -411,26 +406,22 @@
     )(parts, own_queries, new_rows)
     heads = exchange(heads)
 
-    half = (owners * own, out_columns)
-    keep, send = pl.pallas_call(
+    part = pl.pallas_call(
         output_kernel,
-        out_shape=(jax.ShapeDtypeStruct(half, f32), jax.ShapeDtypeStruct(half, bf16)),
-        in_specs=[SMEM, VMEM, VMEM],
-        out_specs=(VMEM, VMEM),
+        out_shape=jax.ShapeDtypeStruct((steps, requests, out_columns), bf16),
+        in_specs=[VMEM, VMEM],
+        out_specs=VMEM,
         compiler_params=params(),
-    )(core.reshape(1), heads, w_out)
+    )(heads, w_out)
 
     devices = lax.axis_size("tp")
 
     def swap(x, bits):
         return lax.ppermute(x, "tp", [(i, i ^ bits) for i in range(devices)])
 
-    mine = (keep + swap(send, 1).astype(f32)).astype(bf16)
-    others = [swap(mine, bits) for bits in (2, 6, 4)]
-    near, across, far = (x.astype(f32) for x in others)
-    mine = ((mine.astype(f32) + near) + (across + far)).astype(bf16)
-    other = swap(mine, 1)
-    return jnp.where(core == 0, jnp.stack([mine, other]), jnp.stack([other, mine]))
+    near, across, far = (swap(part, bits).astype(f32) for bits in (2, 6, 4))
+    chips = ((part.astype(f32) + near) + (across + far)).astype(bf16)
+    return (chips.astype(f32) + swap(chips, 1).astype(f32)).astype(bf16)
 
 
 def solution(mesh):

time: 82.6 us -> 82.3 us (level)
    ppermute x5 -> x4, waiting for transfers between devices: 7.51 us -> 7.22 us  [swap(): return lax.ppermute(x, 'tp', [(i, i ^ bits) for i in range(devices)])]
    ppermute x5 -> x4, starting transfers between devices: 10.8 us -> 10.8 us  [swap(): return lax.ppermute(x, 'tp', [(i, i ^ bits) for i in range(devices)])]
  transfers between devices with their start and end apart: 5 -> 4, of which waited for: 5 -> 4; matrix products, arithmetic and copies ran while one was open for 0% -> 0% of each run, Pallas kernels for 0% -> 0%
where the time goes in v6:
time: 82.3 us; the launch traced here: 82 us
  blocking collectives  56.9 us (69%)
  starting transfers between devices  10.8 us (13%)
  waiting for transfers between devices  7.22 us (9%)
  Pallas kernels  6.06 us (7%)
  other arithmetic  0.96 us (1%)
    all_to_all x4, blocking collectives, exchange(): return lax.all_to_all(x, 'kvp', 0, 0, tiled=True)  56.9 us
    ppermute x4, starting transfers between devices, swap(): return lax.ppermute(x, 'tp', [(i, i ^ bits) for i in range(devices)])  10.8 us
    ppermute x4, waiting for transfers between devices, swap(): return lax.ppermute(x, 'tp', [(i, i ^ bits) for i in range(devices)])  7.22 us
    pallas_call x1, Pallas kernels, local(): pl.pallas_call(functools.partial(attention_kernel, scaling, batch), out_s...  2.62 us
    pallas_call x1, Pallas kernels, local(): pl.pallas_call(project_kernel, out_shape=(jax.ShapeDtypeStruct((owners, r...  1.93 us
  transfers between devices with their start and end apart: 4, of which 4 were waited for; matrix products, arithmetic and copies ran while one was open for 0% of the time, Pallas kernels for 0%

profile of v6, /device:TPU:1, one launch (start us, length us, event | category | flops | bytes accessed | tf_op | source)
XLA Modules:
  0.0 82.0 jit_solution(13209144036284361267)
XLA Ops:
  0.0 1.9 %shard_map.100 = (bf16[16,16,1280]{2,1,0:T(8,128)(2,1)S(1)}, f32[16,128]{1,0:T(8,128)S(1)}) custom-call(s32[128]{0:T(128)} %position_hbm.1, bf16[2,128,512]{2,1,0:T(8,128)(2,1)} %hidden_hbm.1, bf16[512,1024]{1,0:T(8,128)(2,1)} %wq_hbm.1, bf16[512,128]{1,0:T(8,128)(2,1)} %wk_hbm.1, bf16[512,128]{1,0:T(8,128)(2,1)} %wv_hbm.1), custom_call_target="tpu_custom_call" | custom-call | tf_op jit(solution)/shard_map/pallas_call | solution.py:348
  1.9 0.1 multiply_sine_fusion
  2.0 20.2 %all_to_all.20.parts_ref = bf16[16,16,1280]{2,1,0:T(8,128)(2,1)S(1)} all-to-all(bf16[16,16,1280]{2,1,0:T(8,128)(2,1)S(1)} %get-tuple-element.15), channel_id=1, replica_groups=mesh['kvp'=16,'tp'=8] {'kvp'}, dimensions={0} | all-to-all | bytes 1310720 | tf_op jit(solution)/shard_map/all_to_all | solution.py:345
  22.2 0.0 copy-start
  22.2 0.0 copy-start.1
  22.2 0.0 copy-start.3
  22.2 0.0 copy-start.4
  22.2 0.2 shard_map.101
  22.4 12.7 %all_to_all.21 = bf16[16,128,128]{2,1,0:T(8,128)(2,1)S(1)} all-to-all(bf16[16,128,128]{2,1,0:T(8,128)(2,1)S(1)} %get-tuple-element.18), channel_id=1, replica_groups=mesh['kvp'=16,'tp'=8] {'kvp'}, dimensions={0} | all-to-all | bytes 1048576 | tf_op jit(solution)/shard_map/all_to_all | solution.py:345
  35.2 0.0 copy-done
  35.2 0.0 copy-done.1
  35.2 0.0 copy-done.3
  35.2 0.0 copy-done.4
  35.2 0.0 copy-start.2
  35.2 2.6 %shard_map.102 = bf16[16,144,128]{2,1,0:T(8,128)(2,1)S(1)} custom-call(s32[64]{0:T(128)S(1)} %copy-done.3, s32[64]{0:T(128)S(1)} %copy-done.4, bf16[128,16,128]{2,1,0:T(8,128)(2,1)S(1)} %bitcast.1, bf16[64,256,128]{2,1,0:T(8,128)(2,1)S(1)} %copy-done, bf16[64,256,128]{2,1,0:T(8,128)(2,1)S(1)} %copy-done.1), custom_call_target="tpu_custom_call" | custom-call | tf_op jit(solution)/shard_map/pallas_call | solution.py:385
  37.8 11.9 %all_to_all.22.parts_ref = bf16[16,144,128]{2,1,0:T(8,128)(2,1)S(1)} all-to-all(bf16[16,144,128]{2,1,0:T(8,128)(2,1)S(1)} %shard_map.102), channel_id=1, replica_groups=mesh['kvp'=16,'tp'=8] {'kvp'}, dimensions={0} | all-to-all | bytes 1179648 | tf_op jit(solution)/shard_map/all_to_all | solution.py:345
  49.7 0.9 %shard_map.103 = bf16[16,16,1024]{2,1,0:T(8,128)(2,1)S(1)} custom-call(bf16[16,144,128]{2,1,0:T(8,128)(2,1)S(1)} %all_to_all.22.parts_ref, bf16[128,128]{1,0:T(8,128)(2,1)S(1)} %get-tuple-element.19.q_ref, bf16[2,16,128]{2,1,0:T(8,128)(2,1)S(1)} %get-tuple-element.20.new_ref), custom_call_target="tpu_custom_call" | custom-call | tf_op jit(solution)/shard_map/pallas_call | solution.py:399
  50.6 12.0 %all_to_all.23.heads_ref = bf16[16,16,1024]{2,1,0:T(8,128)(2,1)S(1)} all-to-all(bf16[16,16,1024]{2,1,0:T(8,128)(2,1)S(1)} %shard_map.103), channel_id=1, replica_groups=mesh['kvp'=16,'tp'=8] {'kvp'}, dimensions={0} | all-to-all | bytes 1048576 | tf_op jit(solution)/shard_map/all_to_all | solution.py:345
  62.7 0.0 copy-done.2
  62.7 0.4 shard_map.104
  63.1 2.8 %collective-permute-start.2 = (bf16[2,128,512]{2,1,0:T(8,128)(2,1)S(1)}, bf16[2,128,512]{2,1,0:T(8,128)(2,1)S(1)}, u32[]{:S(2)}, u32[]{:S(2)}) collective-permute-start(bf16[2,128,512]{2,1,0:T(8,128)(2,1)S(1)} %shard_map.104), channel_id=1, source_target_pairs={{0,4},{1,5},{2,6},{3,7},{4,0},{5,1},{6,2},{7,3},{8,12},{9,13},{10,... | collective-permute-start | bytes 786440 | tf_op jit(solution)/shard_map/ppermute | solution.py:420
  66.0 0.9 %collective-permute-start.1 = (bf16[2,128,512]{2,1,0:T(8,128)(2,1)S(1)}, bf16[2,128,512]{2,1,0:T(8,128)(2,1)S(1)}, u32[]{:S(2)}, u32[]{:S(2)}) collective-permute-start(bf16[2,128,512]{2,1,0:T(8,128)(2,1)S(1)} %shard_map.104), channel_id=1, source_target_pairs={{0,6},{1,7},{2,4},{3,5},{4,2},{5,3},{6,0},{7,1},{8,14},{9,15},{10,... | collective-permute-start | bytes 786440 | tf_op jit(solution)/shard_map/ppermute | solution.py:420
  66.8 0.0 collective-permute-start
  66.8 3.2 %collective-permute-done.2 = bf16[2,128,512]{2,1,0:T(8,128)(2,1)S(1)} collective-permute-done((bf16[2,128,512]{2,1,0:T(8,128)(2,1)S(1)}, bf16[2,128,512]{2,1,0:T(8,128)(2,1)S(1)}, u32[]{:S(2)}, u32[]{:S(2)}) %collective-permute-start.2) | collective-permute-done | bytes 262176 | tf_op jit(solution)/shard_map/ppermute | solution.py:420
  70.0 2.8 %collective-permute-done.1 = bf16[2,128,512]{2,1,0:T(8,128)(2,1)S(1)} collective-permute-done((bf16[2,128,512]{2,1,0:T(8,128)(2,1)S(1)}, bf16[2,128,512]{2,1,0:T(8,128)(2,1)S(1)}, u32[]{:S(2)}, u32[]{:S(2)}) %collective-permute-start.1) | collective-permute-done | bytes 262176 | tf_op jit(solution)/shard_map/ppermute | solution.py:420
  72.8 0.1 collective-permute-done
  72.9 0.1 add_convert_fusion.1
  73.0 7.1 %collective-permute-start.3 = (bf16[2,128,512]{2,1,0:T(8,128)(2,1)S(1)}, bf16[2,128,512]{2,1,0:T(8,128)(2,1)S(1)}, u32[]{:S(2)}, u32[]{:S(2)}) collective-permute-start(bf16[2,128,512]{2,1,0:T(8,128)(2,1)S(1)} %add_convert_fusion.1), channel_id=1, source_target_pairs={{0,1},{1,0},{2,3},{3,2},{4,5},{5,4},{6,7},{7,6},{8,9},{9,8},{10,11... | collective-permute-start | bytes 786440 | tf_op jit(solution)/shard_map/ppermute | solution.py:420
  80.1 1.2 %collective-permute-done.3 = bf16[2,128,512]{2,1,0:T(8,128)(2,1)S(1)} collective-permute-done((bf16[2,128,512]{2,1,0:T(8,128)(2,1)S(1)}, bf16[2,128,512]{2,1,0:T(8,128)(2,1)S(1)}, u32[]{:S(2)}, u32[]{:S(2)}) %collective-permute-start.3) | collective-permute-done | bytes 262176 | tf_op jit(solution)/shard_map/ppermute | solution.py:420
  81.3 0.8 add_convert_fusion
  (1 shorter events, 0.0 us)
Async XLA Ops:
  22.2 13.0 %copy-start = (bf16[64,256,128]{2,1,0:T(8,128)(2,1)S(1)}, bf16[64,256,128]{2,1,0:T(8,128)(2,1)}, u32[]{:S(2)}) copy-start(bf16[64,256,128]{2,1,0:T(8,128)(2,1)} %k_ref.1) | copy-start | bytes 12582916
  22.2 13.0 %copy-start.1 = (bf16[64,256,128]{2,1,0:T(8,128)(2,1)S(1)}, bf16[64,256,128]{2,1,0:T(8,128)(2,1)}, u32[]{:S(2)}) copy-start(bf16[64,256,128]{2,1,0:T(8,128)(2,1)} %v_ref.1) | copy-start | bytes 12582916
  22.2 13.0 %copy-start.3 = (s32[64]{0:T(128)S(1)}, s32[64]{0:T(128)}, u32[]{:S(2)}) copy-start(s32[64]{0:T(128)} %request_ref.1) | copy-start | bytes 772
  22.2 13.0 %copy-start.4 = (s32[64]{0:T(128)S(1)}, s32[64]{0:T(128)}, u32[]{:S(2)}) copy-start(s32[64]{0:T(128)} %fill_ref.1) | copy-start | bytes 772
  35.2 27.5 %copy-start.2 = (bf16[1024,512]{1,0:T(8,128)(2,1)S(1)}, bf16[1024,512]{1,0:T(8,128)(2,1)}, u32[]{:S(2)}) copy-start(bf16[1024,512]{1,0:T(8,128)(2,1)} %w_ref.1) | copy-start | bytes 3145732
  63.1 6.8 %collective-permute-start.2 = (bf16[2,128,512]{2,1,0:T(8,128)(2,1)S(1)}, bf16[2,128,512]{2,1,0:T(8,128)(2,1)S(1)}, u32[]{:S(2)}, u32[]{:S(2)}) collective-permute-start(bf16[2,128,512]{2,1,0:T(8,128)(2,1)S(1)} %shard_map.104), channel_id=1, source_target_pairs={{0,4},{1,5},{2,6},{3,7},{4,0},{5,1},{6,2},{7,3},{8,12},{9,13},{10,... | collective-permute-start | bytes 786440 | tf_op jit(solution)/shard_map/ppermute | solution.py:420
  66.0 6.8 %collective-permute-start.1 = (bf16[2,128,512]{2,1,0:T(8,128)(2,1)S(1)}, bf16[2,128,512]{2,1,0:T(8,128)(2,1)S(1)}, u32[]{:S(2)}, u32[]{:S(2)}) collective-permute-start(bf16[2,128,512]{2,1,0:T(8,128)(2,1)S(1)} %shard_map.104), channel_id=1, source_target_pairs={{0,6},{1,7},{2,4},{3,5},{4,2},{5,3},{6,0},{7,1},{8,14},{9,15},{10,... | collective-permute-start | bytes 786440 | tf_op jit(solution)/shard_map/ppermute | solution.py:420
  66.8 6.1 %collective-permute-start = (bf16[2,128,512]{2,1,0:T(8,128)(2,1)S(1)}, bf16[2,128,512]{2,1,0:T(8,128)(2,1)S(1)}, u32[]{:S(2)}, u32[]{:S(2)}) collective-permute-start(bf16[2,128,512]{2,1,0:T(8,128)(2,1)S(1)} %shard_map.104), channel_id=1, source_target_pairs={{0,2},{1,3},{2,0},{3,1},{4,6},{5,7},{6,4},{7,5},{8,10},{9,11},{10,... | collective-permute-start | bytes 786440 | tf_op jit(solution)/shard_map/ppermute | solution.py:420
  73.0 8.2 %collective-permute-start.3 = (bf16[2,128,512]{2,1,0:T(8,128)(2,1)S(1)}, bf16[2,128,512]{2,1,0:T(8,128)(2,1)S(1)}, u32[]{:S(2)}, u32[]{:S(2)}) collective-permute-start(bf16[2,128,512]{2,1,0:T(8,128)(2,1)S(1)} %add_convert_fusion.1), channel_id=1, source_target_pairs={{0,1},{1,0},{2,3},{3,2},{4,5},{5,4},{6,7},{7,6},{8,9},{9,8},{10,11... | collective-permute-start | bytes 786440 | tf_op jit(solution)/shard_map/ppermute | solution.py:420

commit v7 on v6

--- a/solution.py
+++ b/solution.py
@@ -65,18 +65,19 @@
     ]
     for copy in copies:
         copy.start()
-    first = lax.axis_index("kvp") * own
-    copies[0].wait()
-    row = lax.broadcasted_iota(jnp.int32, (rows, HEAD_SIZE), 0)
-    slots = jnp.zeros((rows, HEAD_SIZE), jnp.int32)
-    for r in range(own):
-        slots = jnp.where(row % own == r, position_ref[first + r], slots)
-    slot_ref[...] = (slots + row // own).astype(jnp.float32)
     copies[1].wait()
     hidden = hidden_ref[...].reshape(steps * requests, width)
     queries = wq_ref.shape[1]
     starts = (queries, queries + wk_ref.shape[1], 0)
     for copy, ref, column in zip(copies[2:], targets[2:], starts):
+        if ref is wq_ref:
+            first = lax.axis_index("kvp") * own
+            copies[0].wait()
+            row = lax.broadcasted_iota(jnp.int32, (rows, HEAD_SIZE), 0)
+            slots = jnp.zeros((rows, HEAD_SIZE), jnp.int32)
+            for r in range(own):
+                slots = jnp.where(row % own == r, position_ref[first + r], slots)
+            slot_ref[...] = (slots + row // own).astype(jnp.float32)
         copy.wait()
         total = ref.shape[1]
         chunk = min(total, 256)

time: 82.3 us -> 82.3 us (level)
  no operation moved by 1% of the time
where the time goes in v7:
time: 82.3 us; the launch traced here: 82 us
  blocking collectives  56.9 us (69%)
  starting transfers between devices  10.8 us (13%)
  waiting for transfers between devices  7.2 us (9%)
  Pallas kernels  6.06 us (7%)
  other arithmetic  0.96 us (1%)
    all_to_all x4, blocking collectives, exchange(): return lax.all_to_all(x, 'kvp', 0, 0, tiled=True)  56.9 us
    ppermute x4, starting transfers between devices, swap(): return lax.ppermute(x, 'tp', [(i, i ^ bits) for i in range(devices)])  10.8 us
    ppermute x4, waiting for transfers between devices, swap(): return lax.ppermute(x, 'tp', [(i, i ^ bits) for i in range(devices)])  7.2 us
    pallas_call x1, Pallas kernels, local(): pl.pallas_call(functools.partial(attention_kernel, scaling, batch), out_s...  2.61 us
    pallas_call x1, Pallas kernels, local(): pl.pallas_call(project_kernel, out_shape=(jax.ShapeDtypeStruct((owners, r...  1.93 us
  transfers between devices with their start and end apart: 4, of which 4 were waited for; matrix products, arithmetic and copies ran while one was open for 0% of the time, Pallas kernels for 0%

profile of v7, /device:TPU:1, one launch (start us, length us, event | category | flops | bytes accessed | tf_op | source)
XLA Modules:
  0.0 82.0 jit_solution(13258988061433132959)
XLA Ops:
  0.0 1.9 %shard_map.100 = (bf16[16,16,1280]{2,1,0:T(8,128)(2,1)S(1)}, f32[16,128]{1,0:T(8,128)S(1)}) custom-call(s32[128]{0:T(128)} %position_hbm.1, bf16[2,128,512]{2,1,0:T(8,128)(2,1)} %hidden_hbm.1, bf16[512,1024]{1,0:T(8,128)(2,1)} %wq_hbm.1, bf16[512,128]{1,0:T(8,128)(2,1)} %wk_hbm.1, bf16[512,128]{1,0:T(8,128)(2,1)} %wv_hbm.1), custom_call_target="tpu_custom_call" | custom-call | tf_op jit(solution)/shard_map/pallas_call | solution.py:349
  1.9 0.1 multiply_sine_fusion
  2.0 20.2 %all_to_all.20.parts_ref = bf16[16,16,1280]{2,1,0:T(8,128)(2,1)S(1)} all-to-all(bf16[16,16,1280]{2,1,0:T(8,128)(2,1)S(1)} %get-tuple-element.15), channel_id=1, replica_groups=mesh['kvp'=16,'tp'=8] {'kvp'}, dimensions={0} | all-to-all | bytes 1310720 | tf_op jit(solution)/shard_map/all_to_all | solution.py:346
  22.2 0.0 copy-start
  22.2 0.0 copy-start.1
  22.2 0.0 copy-start.3
  22.2 0.0 copy-start.4
  22.2 0.2 shard_map.101
  22.4 12.7 %all_to_all.21 = bf16[16,128,128]{2,1,0:T(8,128)(2,1)S(1)} all-to-all(bf16[16,128,128]{2,1,0:T(8,128)(2,1)S(1)} %get-tuple-element.18), channel_id=1, replica_groups=mesh['kvp'=16,'tp'=8] {'kvp'}, dimensions={0} | all-to-all | bytes 1048576 | tf_op jit(solution)/shard_map/all_to_all | solution.py:346
  35.2 0.0 copy-done
  35.2 0.0 copy-done.1
  35.2 0.0 copy-done.3
  35.2 0.0 copy-done.4
  35.2 0.0 copy-start.2
  35.2 2.6 %shard_map.102 = bf16[16,144,128]{2,1,0:T(8,128)(2,1)S(1)} custom-call(s32[64]{0:T(128)S(1)} %copy-done.3, s32[64]{0:T(128)S(1)} %copy-done.4, bf16[128,16,128]{2,1,0:T(8,128)(2,1)S(1)} %bitcast.1, bf16[64,256,128]{2,1,0:T(8,128)(2,1)S(1)} %copy-done, bf16[64,256,128]{2,1,0:T(8,128)(2,1)S(1)} %copy-done.1), custom_call_target="tpu_custom_call" | custom-call | tf_op jit(solution)/shard_map/pallas_call | solution.py:386
  37.8 11.9 %all_to_all.22.parts_ref = bf16[16,144,128]{2,1,0:T(8,128)(2,1)S(1)} all-to-all(bf16[16,144,128]{2,1,0:T(8,128)(2,1)S(1)} %shard_map.102), channel_id=1, replica_groups=mesh['kvp'=16,'tp'=8] {'kvp'}, dimensions={0} | all-to-all | bytes 1179648 | tf_op jit(solution)/shard_map/all_to_all | solution.py:346
  49.7 0.9 %shard_map.103 = bf16[16,16,1024]{2,1,0:T(8,128)(2,1)S(1)} custom-call(bf16[16,144,128]{2,1,0:T(8,128)(2,1)S(1)} %all_to_all.22.parts_ref, bf16[128,128]{1,0:T(8,128)(2,1)S(1)} %get-tuple-element.19.q_ref, bf16[2,16,128]{2,1,0:T(8,128)(2,1)S(1)} %get-tuple-element.20.new_ref), custom_call_target="tpu_custom_call" | custom-call | tf_op jit(solution)/shard_map/pallas_call | solution.py:400
  50.6 12.0 %all_to_all.23.heads_ref = bf16[16,16,1024]{2,1,0:T(8,128)(2,1)S(1)} all-to-all(bf16[16,16,1024]{2,1,0:T(8,128)(2,1)S(1)} %shard_map.103), channel_id=1, replica_groups=mesh['kvp'=16,'tp'=8] {'kvp'}, dimensions={0} | all-to-all | bytes 1048576 | tf_op jit(solution)/shard_map/all_to_all | solution.py:346
  62.7 0.0 copy-done.2
  62.7 0.4 shard_map.104
  63.1 2.8 %collective-permute-start.2 = (bf16[2,128,512]{2,1,0:T(8,128)(2,1)S(1)}, bf16[2,128,512]{2,1,0:T(8,128)(2,1)S(1)}, u32[]{:S(2)}, u32[]{:S(2)}) collective-permute-start(bf16[2,128,512]{2,1,0:T(8,128)(2,1)S(1)} %shard_map.104), channel_id=1, source_target_pairs={{0,4},{1,5},{2,6},{3,7},{4,0},{5,1},{6,2},{7,3},{8,12},{9,13},{10,... | collective-permute-start | bytes 786440 | tf_op jit(solution)/shard_map/ppermute | solution.py:421
  65.9 0.9 %collective-permute-start.1 = (bf16[2,128,512]{2,1,0:T(8,128)(2,1)S(1)}, bf16[2,128,512]{2,1,0:T(8,128)(2,1)S(1)}, u32[]{:S(2)}, u32[]{:S(2)}) collective-permute-start(bf16[2,128,512]{2,1,0:T(8,128)(2,1)S(1)} %shard_map.104), channel_id=1, source_target_pairs={{0,6},{1,7},{2,4},{3,5},{4,2},{5,3},{6,0},{7,1},{8,14},{9,15},{10,... | collective-permute-start | bytes 786440 | tf_op jit(solution)/shard_map/ppermute | solution.py:421
  66.8 0.0 collective-permute-start
  66.8 3.2 %collective-permute-done.2 = bf16[2,128,512]{2,1,0:T(8,128)(2,1)S(1)} collective-permute-done((bf16[2,128,512]{2,1,0:T(8,128)(2,1)S(1)}, bf16[2,128,512]{2,1,0:T(8,128)(2,1)S(1)}, u32[]{:S(2)}, u32[]{:S(2)}) %collective-permute-start.2) | collective-permute-done | bytes 262176 | tf_op jit(solution)/shard_map/ppermute | solution.py:421
  70.0 2.8 %collective-permute-done.1 = bf16[2,128,512]{2,1,0:T(8,128)(2,1)S(1)} collective-permute-done((bf16[2,128,512]{2,1,0:T(8,128)(2,1)S(1)}, bf16[2,128,512]{2,1,0:T(8,128)(2,1)S(1)}, u32[]{:S(2)}, u32[]{:S(2)}) %collective-permute-start.1) | collective-permute-done | bytes 262176 | tf_op jit(solution)/shard_map/ppermute | solution.py:421
  72.7 0.1 collective-permute-done
  72.9 0.1 add_convert_fusion.1
  73.0 7.1 %collective-permute-start.3 = (bf16[2,128,512]{2,1,0:T(8,128)(2,1)S(1)}, bf16[2,128,512]{2,1,0:T(8,128)(2,1)S(1)}, u32[]{:S(2)}, u32[]{:S(2)}) collective-permute-start(bf16[2,128,512]{2,1,0:T(8,128)(2,1)S(1)} %add_convert_fusion.1), channel_id=1, source_target_pairs={{0,1},{1,0},{2,3},{3,2},{4,5},{5,4},{6,7},{7,6},{8,9},{9,8},{10,11... | collective-permute-start | bytes 786440 | tf_op jit(solution)/shard_map/ppermute | solution.py:421
  80.1 1.2 %collective-permute-done.3 = bf16[2,128,512]{2,1,0:T(8,128)(2,1)S(1)} collective-permute-done((bf16[2,128,512]{2,1,0:T(8,128)(2,1)S(1)}, bf16[2,128,512]{2,1,0:T(8,128)(2,1)S(1)}, u32[]{:S(2)}, u32[]{:S(2)}) %collective-permute-start.3) | collective-permute-done | bytes 262176 | tf_op jit(solution)/shard_map/ppermute | solution.py:421
  81.3 0.8 add_convert_fusion
  (1 shorter events, 0.0 us)
Async XLA Ops:
  22.2 12.9 %copy-start = (bf16[64,256,128]{2,1,0:T(8,128)(2,1)S(1)}, bf16[64,256,128]{2,1,0:T(8,128)(2,1)}, u32[]{:S(2)}) copy-start(bf16[64,256,128]{2,1,0:T(8,128)(2,1)} %k_ref.1) | copy-start | bytes 12582916
  22.2 12.9 %copy-start.1 = (bf16[64,256,128]{2,1,0:T(8,128)(2,1)S(1)}, bf16[64,256,128]{2,1,0:T(8,128)(2,1)}, u32[]{:S(2)}) copy-start(bf16[64,256,128]{2,1,0:T(8,128)(2,1)} %v_ref.1) | copy-start | bytes 12582916
  22.2 12.9 %copy-start.3 = (s32[64]{0:T(128)S(1)}, s32[64]{0:T(128)}, u32[]{:S(2)}) copy-start(s32[64]{0:T(128)} %request_ref.1) | copy-start | bytes 772
  22.2 13.0 %copy-start.4 = (s32[64]{0:T(128)S(1)}, s32[64]{0:T(128)}, u32[]{:S(2)}) copy-start(s32[64]{0:T(128)} %fill_ref.1) | copy-start | bytes 772
  35.2 27.5 %copy-start.2 = (bf16[1024,512]{1,0:T(8,128)(2,1)S(1)}, bf16[1024,512]{1,0:T(8,128)(2,1)}, u32[]{:S(2)}) copy-start(bf16[1024,512]{1,0:T(8,128)(2,1)} %w_ref.1) | copy-start | bytes 3145732
  63.1 6.8 %collective-permute-start.2 = (bf16[2,128,512]{2,1,0:T(8,128)(2,1)S(1)}, bf16[2,128,512]{2,1,0:T(8,128)(2,1)S(1)}, u32[]{:S(2)}, u32[]{:S(2)}) collective-permute-start(bf16[2,128,512]{2,1,0:T(8,128)(2,1)S(1)} %shard_map.104), channel_id=1, source_target_pairs={{0,4},{1,5},{2,6},{3,7},{4,0},{5,1},{6,2},{7,3},{8,12},{9,13},{10,... | collective-permute-start | bytes 786440 | tf_op jit(solution)/shard_map/ppermute | solution.py:421
  65.9 6.8 %collective-permute-start.1 = (bf16[2,128,512]{2,1,0:T(8,128)(2,1)S(1)}, bf16[2,128,512]{2,1,0:T(8,128)(2,1)S(1)}, u32[]{:S(2)}, u32[]{:S(2)}) collective-permute-start(bf16[2,128,512]{2,1,0:T(8,128)(2,1)S(1)} %shard_map.104), channel_id=1, source_target_pairs={{0,6},{1,7},{2,4},{3,5},{4,2},{5,3},{6,0},{7,1},{8,14},{9,15},{10,... | collective-permute-start | bytes 786440 | tf_op jit(solution)/shard_map/ppermute | solution.py:421
  66.8 6.0 %collective-permute-start = (bf16[2,128,512]{2,1,0:T(8,128)(2,1)S(1)}, bf16[2,128,512]{2,1,0:T(8,128)(2,1)S(1)}, u32[]{:S(2)}, u32[]{:S(2)}) collective-permute-start(bf16[2,128,512]{2,1,0:T(8,128)(2,1)S(1)} %shard_map.104), channel_id=1, source_target_pairs={{0,2},{1,3},{2,0},{3,1},{4,6},{5,7},{6,4},{7,5},{8,10},{9,11},{10,... | collective-permute-start | bytes 786440 | tf_op jit(solution)/shard_map/ppermute | solution.py:421
  73.0 8.3 %collective-permute-start.3 = (bf16[2,128,512]{2,1,0:T(8,128)(2,1)S(1)}, bf16[2,128,512]{2,1,0:T(8,128)(2,1)S(1)}, u32[]{:S(2)}, u32[]{:S(2)}) collective-permute-start(bf16[2,128,512]{2,1,0:T(8,128)(2,1)S(1)} %add_convert_fusion.1), channel_id=1, source_target_pairs={{0,1},{1,0},{2,3},{3,2},{4,5},{5,4},{6,7},{7,6},{8,9},{9,8},{10,11... | collective-permute-start | bytes 786440 | tf_op jit(solution)/shard_map/ppermute | solution.py:421
